TPU v7x, 128 devices: a whole 4x4x4 slice. The times are simulated.
128 devices in a mesh: group: 8 (over z, core), dev: 16 (over y, x).
Axes of the slice: x: 4, y: 4, z: 4, core: 2. Of those that a mesh axis runs over, the one named last changes fastest.
Arguments:
- positions: float32 [3, 4194304], P(None, ('group', 'dev')), may hold values from -0.5 to 2.5
- right_sides: float32 [8, 4194304], P(None, ('group', 'dev')), may hold values from -6 to 6
- leaf_basis: bfloat16 [16384, 64, 256], P(('group', 'dev')), may hold values from -0.375 to 0.375
- leaf_transfer: bfloat16 [64, 1048576], P(None, ('group', 'dev')), may hold values from -0.75 to 0.75
- far_coupling: bfloat16 [128, 128, 64, 384], P(('group', 'dev')), may hold values from -0.3125 to 0.3125
- top_transfer: float32 [254, 4096], replicated, may hold values from -0.5 to 0.5
- top_coupling: float32 [254, 4096], replicated, may hold values from -0.75 to 0.75
- near_list: int32 [16384, 6], P(('group', 'dev')), may hold values from 0 to 255, as said below
- send_leaf: int32 [128, 128, 6], P(('group', 'dev')), may hold values from 0 to 127
- send_count: int32 [128, 128], P(('group', 'dev')), may hold values from 1 to 6, as said below
- far_target: int32 [128, 128, 6], P(('group', 'dev')), may hold values from 0 to 127
Outputs:
- potential: float32 [8, 4194304], P(None, ('group', 'dev'))
Inputs may be any that keep to these rules, and one draw needn't show every extreme that they name: `near_list`: every one of the 256 leaves that a device sees is named in its rows of the list. `send_count`: every sender fills all 6 slots of its message to one receiver, and every receiver gets one full message.
All inputs are finite; a program needn't handle non-finite values.
Results may differ from a plain program's by a relative error of at most 0.0042.
Values may be sent and summed in bfloat16 or wider, within the bound.
No kernel may reach another device: no remote copies, remote signals or barrier semaphores. Data moves between devices by JAX's collectives and lax.ppermute only.
A program may use at most 128 MiB of HBM per device.

v0:
```python
import math

import jax
import jax.numpy as jnp
from jax import lax
from jax.sharding import PartitionSpec as P

EDGE = 64


kernel_scale = 0.25 / (4.0 * math.pi)
smoothing = 0.0025


def partner(value, axis, apart):
    mask = 2**apart
    pairs = [(source, source ^ mask) for source in range(lax.axis_size(axis))]
    return lax.ppermute(value, axis, pairs)


def from_behind(block, axis, distance):
    devices = range(lax.axis_size(axis))
    route = [(i - distance, i) for i in devices if i - distance in devices]
    return lax.ppermute(block, axis, route)


def near_field(own_points, seen_points, seen_values, near_rows):
    leaves = near_rows.shape[0]
    group_size = math.gcd(leaves, 8)
    leaf_width = own_points.shape[2]

    def one_group(first_leaf):
        picked = lax.dynamic_slice_in_dim(near_rows, first_leaf, group_size, 0)
        target_points = lax.dynamic_slice_in_dim(own_points, first_leaf, group_size, 1)
        source_points = seen_points[:, picked]
        source_values = seen_values[:, picked]
        distance = jnp.zeros(picked.shape + (leaf_width, leaf_width), jnp.float32)
        for component in range(3):
            difference = (
                target_points[component][:, None, :, None] - source_points[component][:, :, None, :]
            )
            distance = distance + difference * difference
        kernel = (kernel_scale / jnp.sqrt(distance + smoothing)).astype(jnp.bfloat16)
        return jnp.einsum(
            "gkpq,ngkq->ngp", kernel, source_values, preferred_element_type=jnp.float32
        )

    starts = jnp.arange(leaves // group_size, dtype=jnp.int32) * group_size
    blocks = lax.map(one_group, starts)
    return blocks.transpose(1, 0, 2, 3).reshape(seen_values.shape[0], leaves, leaf_width)


def shards(
    positions,
    right_sides,
    leaf_basis,
    leaf_transfer,
    far_coupling,
    top_transfer,
    top_coupling,
    near_list,
    send_leaf,
    send_count,
    far_target,
):
    highest = lax.Precision.HIGHEST
    rhs_count, point_count = right_sides.shape
    leaves, rank, leaf_width = leaf_basis.shape
    slot_count = send_leaf.shape[2]
    group_count = lax.axis_size("group")
    group_devices = lax.axis_size("dev")
    owners = group_count * group_devices
    owner_index = lax.axis_index("group") * group_devices + lax.axis_index("dev")
    levels = owners.bit_length() - 1
    dev_bits = group_devices.bit_length() - 1
    rounded_values = right_sides.astype(jnp.bfloat16)
    moments = jnp.einsum(
        "lrp,nlp->lnr",
        leaf_basis,
        rounded_values.reshape(rhs_count, leaves, leaf_width),
        preferred_element_type=jnp.float32,
    ).astype(jnp.bfloat16)
    transfer_leaf = leaf_transfer.reshape(rank, leaves, rank)
    device_moment = jnp.einsum(
        "lnb,bla->na", moments, transfer_leaf, preferred_element_type=jnp.float32
    )
    device_moment = device_moment * (1.0 / math.sqrt(leaves))
    flat_moments = moments.reshape(leaves, rhs_count * rank)
    chosen = flat_moments[send_leaf[0]]
    live_slots = jnp.arange(slot_count, dtype=jnp.int32)[None, :] < send_count[0][:, None]
    outgoing = jnp.where(live_slots[:, :, None], chosen, jnp.zeros((), jnp.bfloat16))
    incoming = lax.all_to_all(outgoing, ("group", "dev"), split_axis=0, concat_axis=0, tiled=True)
    transfer_table = top_transfer.reshape(-1, rank, rank)
    coupling_table = top_coupling.reshape(-1, rank, rank)
    sibling_moments = []
    current = device_moment
    for level_index in range(levels):
        if level_index < dev_bits:
            sibling = partner(current, "dev", level_index)
        else:
            sibling = partner(current, "group", level_index - dev_bits)
        sibling_moments.append(sibling)
        if level_index + 1 < levels:
            cluster = owner_index >> level_index
            node_base = 2 * owners - 2 * (owners >> level_index)
            is_right = cluster & 1 == 1
            left_moment = jnp.where(is_right, sibling, current)
            right_moment = jnp.where(is_right, current, sibling)
            left_node = node_base + cluster - (cluster & 1)
            current = jnp.dot(left_moment, transfer_table[left_node], precision=highest) + jnp.dot(
                right_moment, transfer_table[left_node + 1], precision=highest
            )
    local_field = jnp.zeros((rhs_count, rank), jnp.float32)
    for level_index in reversed(range(levels)):
        cluster = owner_index >> level_index
        node_index = 2 * owners - 2 * (owners >> level_index) + cluster
        coupling_term = jnp.dot(
            sibling_moments[level_index], coupling_table[node_index].T, precision=highest
        )
        local_field = coupling_term + jnp.dot(
            local_field, transfer_table[node_index].T, precision=highest
        )
    device_field = local_field.astype(jnp.bfloat16)
    rim_width = EDGE * leaf_width
    points_below = from_behind(positions[:, point_count - rim_width :], ("group", "dev"), 1)
    points_above = from_behind(positions[:, :rim_width], ("group", "dev"), -1)
    values_below = from_behind(rounded_values[:, point_count - rim_width :], ("group", "dev"), 1)
    values_above = from_behind(rounded_values[:, :rim_width], ("group", "dev"), -1)
    coupling_blocks = far_coupling[0].reshape(owners, rank, slot_count, rank)
    contrib = jnp.einsum(
        "pasb,psnb->psna",
        coupling_blocks,
        incoming.reshape(owners, slot_count, rhs_count, rank),
        preferred_element_type=jnp.float32,
    )
    targets = (
        far_target[0][:, :, None] == jnp.arange(leaves, dtype=jnp.int32)[None, None, :]
    ).astype(jnp.float32)
    far_local = jnp.einsum("psl,psna->lna", targets, contrib, precision=highest)
    device_local = jnp.einsum(
        "bla,na->lnb", transfer_leaf, device_field, preferred_element_type=jnp.float32
    )
    leaf_local = (device_local + far_local).astype(jnp.bfloat16)
    far_potential = jnp.einsum(
        "lbp,lnb->nlp", leaf_basis, leaf_local, preferred_element_type=jnp.float32
    )
    seen_leaves = leaves + 2 * EDGE
    seen_points = jnp.concatenate([points_below, positions, points_above], 1).reshape(
        3, seen_leaves, leaf_width
    )
    seen_values = jnp.concatenate([values_below, rounded_values, values_above], 1).reshape(
        rhs_count, seen_leaves, leaf_width
    )
    own_points = positions.reshape(3, leaves, leaf_width)
    self_rows = (jnp.arange(leaves, dtype=jnp.int32) + EDGE)[:, None]
    near_rows = jnp.concatenate([self_rows, near_list], 1)
    near_potential = near_field(own_points, seen_points, seen_values, near_rows)
    potential = far_potential + near_potential
    return potential.reshape(rhs_count, point_count)


def solution(mesh):
    placed = (
        P(None, ("group", "dev")),
        P(None, ("group", "dev")),
        P(("group", "dev"), None, None),
        P(None, ("group", "dev")),
        P(("group", "dev"), None, None, None),
        P(),
        P(),
        P(("group", "dev"), None),
        P(("group", "dev"), None, None),
        P(("group", "dev"), None),
        P(("group", "dev"), None, None),
    )
    return jax.shard_map(
        shards, mesh=mesh, in_specs=placed, out_specs=P(None, ("group", "dev")), check_vma=False
    )
```

profile of v0, /device:TPU:4, one launch (start us, length us, event | category | flops | bytes accessed | tf_op | source)
XLA Modules:
  0.0 432.5 jit_solution(6873468238381356481)
XLA Ops:
  2.1 2.4 collective-permute-start.8
  4.5 3.4 collective-permute-start.7
  7.9 1.9 fusion.70
  9.9 2.4 collective-permute-start.10
  12.3 4.7 %collective-permute-start.9 = (f32[3,16384]{1,0:T(4,128)}, f32[3,16384]{1,0:T(4,128)}, u32[]{:S(2)}, u32[]{:S(2)}) collective-permute-start(f32[3,16384]{1,0:T(4,128)} %get-tuple-element.95), channel_id=1, source_target_pairs={{0,1},{1,2},{2,3},{3,4},{4,5},{5,6},{6,7},{7,8},{8,9},{9,10},{10,1... | collective-permute-start | bytes 589832 | tf_op jit(solution)/shard_map/ppermute | solution.py:24
  17.0 3.3 reshape.100
  20.3 3.4 convolution_convert_fusion
  23.7 2.3 fusion.29
  26.0 4.1 collective-permute-start
  30.5 6.1 %copy.47 = f32[254,4096]{0,1:T(8,128)} copy(f32[254,4096]{1,0:T(8,128)} %param.18) | data formatting | bytes 8323072 | tf_op args[5]
  36.6 30.3 %dynamic-slice_reduce_fusion = (f32[64,64]{1,0:T(8,128)S(1)}, f32[64,64]{1,0:T(8,128)S(1)}, f32[64,64]{1,0:T(8,128)S(1)}, f32[64,64]{1,0:T(8,128)S(1)}, f32[64,6...) fusion(f32[254,64,64]{0,2,1:T(8,128)} %bitcast.140, ...), kind=kLoop, calls=%fused_computation.21 | loop fusion | bytes 589896 | tf_op jit(solution)/shard_map/dynamic_slice | solution.py:121
  66.9 3.4 dynamic-slice_reduce_fusion.24
  70.6 3.3 gather_fusion.2
  74.0 2.3 reshape.127
  76.6 2.4 broadcast_select_fusion
  79.0 13.7 %all-to-all-start = ((bf16[128,6,512]{2,1,0:T(8,128)(2,1)}), bf16[128,6,512]{2,1,0:T(8,128)(2,1)}, u32[]{:S(2)}, u32[]{:S(2)}) async-start(bf16[128,6,512]{2,1,0:T(8,128)(2,1)} %broadcast_select_fusion), calls=%async_computation | async-start | bytes 2097152 | tf_op jit(solution)/shard_map/all_to_all | solution.py:92
  94.7 5.6 %copy.46 = f32[254,4096]{0,1:T(8,128)} copy(f32[254,4096]{1,0:T(8,128)} %param.19) | data formatting | bytes 8323072 | tf_op args[6]
  100.3 5.1 %collective-permute-done.2 = f32[8,64]{1,0:T(8,128)S(1)} collective-permute-done((f32[8,64]{1,0:T(8,128)S(1)}, f32[8,64]{1,0:T(8,128)S(1)}, u32[]{:S(2)}, u32[]{:S(2)}) %collective-permute-start.2) | collective-permute-done | bytes 2080 | tf_op jit(solution)/shard_map/ppermute | solution.py:18
  105.7 2.8 collective-permute-start.3
  108.5 14.1 %dynamic-slice_reduce_fusion.25 = (f32[64,64]{1,0:T(8,128)}, f32[64,64]{1,0:T(8,128)}, f32[64,64]{1,0:T(8,128)}, f32[64,64]{1,0:T(8,128)}, f32[64,64]{1,0:T(8,128)}, /*index=5*/f32[64,64]{1,0:T(8,128)}, f32[64,64]{1,0:T(8,128)}) fusion(f32[254,64,64]{0,2,1:T(8,128)} %bitcast.142, s32[]{:T(128)S(6)} %select_n.148, s32[]{:T(128)S(6)} %select_n.184, ...), kind=kLoop, calls=%fused_computation.46 | loop fusion | bytes 229404 | tf_op jit(solution)/shard_map/dynamic_slice | solution.py:118
  126.8 1.9 collective-permute-done.5
  128.9 3.5 collective-permute-start.6
  133.8 9.3 %copy.53 = bf16[1,128,64,384]{1,3,2,0:T(8,128)(2,1)} copy(bf16[1,128,64,384]{3,2,1,0:T(8,128)(2,1)} %param.17) | data formatting | bytes 12582912 | tf_op args[4]
  143.1 18.7 %copy.55 = bf16[128,64,6,64]{3,1,2,0:T(8,128)(2,1)} copy(bf16[128,64,6,64]{0,3,2,1:T(8,128)(2,1)} %bitcast.143) | data formatting | bytes 12582912 | tf_op jit(solution)/shard_map/reshape;squeeze | solution.py:129
  165.6 2.3 pad_maximum_fusion.1
  167.9 2.1 pad_maximum_fusion
  170.0 239.8 %while.10 = (s32[]{:T(128)}, f32[16,8,8,256]{3,1,2,0:T(8,128)}, s32[16]{0:T(128)}, s32[128,7]{0,1:T(8,128)S(1)}, bf16[8,256,256]{2,0,1:T(8,128)(2,1)}, /*index=5...) while((s32[]{:T(128)}, f32[16,8,8,256]{3,1,2,0:T(8,128)}, ...), condition=%wide.region_1.2_spmd, body=%wide.region_0.1_spmd.sunk | while | flops 99091632 | bytes 2038391 | solution.py:49
  175.4 1.9 gather_fusion.1
  178.2 6.8 %fusion.129 = f32[16,8,8,256]{3,1,2,0:T(8,128)} fusion(f32[16,8,8,256]{3,1,2,0:T(8,128)} %get-tuple-element.167, s32[]{:T(128)S(6)} %copy.98, bf16[8,8,7,256]{3,0,2,1:T(8,128)(2,1)S(1)} %bitcast.147, f32[8,7,256]{2,1,0:T(8,128)S(1)} %get-tuple-element.148, f32[8,256]{1,0:T(8,128)S(1)} %get-tuple-element.149, ...), kind=kOutput, calls=%fused_computation.6.clone.1 | convolution fusion | flops 99090432 | bytes 491524 | tf_op jit(solution)/shard_map/while/body/eval_jaxpr/gkpq,ngkq->ngp/dot_general | solution.py:44
  188.6 1.8 gather_fusion
  190.4 1.9 gather_fusion.1
  193.2 6.8 %fusion.129 = f32[16,8,8,256]{3,1,2,0:T(8,128)} fusion(f32[16,8,8,256]{3,1,2,0:T(8,128)} %get-tuple-element.167, s32[]{:T(128)S(6)} %copy.98, bf16[8,8,7,256]{3,0,2,1:T(8,128)(2,1)S(1)} %bitcast.147, f32[8,7,256]{2,1,0:T(8,128)S(1)} %get-tuple-element.148, f32[8,256]{1,0:T(8,128)S(1)} %get-tuple-element.149, ...), kind=kOutput, calls=%fused_computation.6.clone.1 | convolution fusion | flops 99090432 | bytes 491524 | tf_op jit(solution)/shard_map/while/body/eval_jaxpr/gkpq,ngkq->ngp/dot_general | solution.py:44
  205.4 1.9 gather_fusion.1
  208.1 6.8 %fusion.129 = f32[16,8,8,256]{3,1,2,0:T(8,128)} fusion(f32[16,8,8,256]{3,1,2,0:T(8,128)} %get-tuple-element.167, s32[]{:T(128)S(6)} %copy.98, bf16[8,8,7,256]{3,0,2,1:T(8,128)(2,1)S(1)} %bitcast.147, f32[8,7,256]{2,1,0:T(8,128)S(1)} %get-tuple-element.148, f32[8,256]{1,0:T(8,128)S(1)} %get-tuple-element.149, ...), kind=kOutput, calls=%fused_computation.6.clone.1 | convolution fusion | flops 99090432 | bytes 491524 | tf_op jit(solution)/shard_map/while/body/eval_jaxpr/gkpq,ngkq->ngp/dot_general | solution.py:44
  220.4 1.9 gather_fusion.1
  223.1 6.8 %fusion.129 = f32[16,8,8,256]{3,1,2,0:T(8,128)} fusion(f32[16,8,8,256]{3,1,2,0:T(8,128)} %get-tuple-element.167, s32[]{:T(128)S(6)} %copy.98, bf16[8,8,7,256]{3,0,2,1:T(8,128)(2,1)S(1)} %bitcast.147, f32[8,7,256]{2,1,0:T(8,128)S(1)} %get-tuple-element.148, f32[8,256]{1,0:T(8,128)S(1)} %get-tuple-element.149, ...), kind=kOutput, calls=%fused_computation.6.clone.1 | convolution fusion | flops 99090432 | bytes 491524 | tf_op jit(solution)/shard_map/while/body/eval_jaxpr/gkpq,ngkq->ngp/dot_general | solution.py:44
  235.4 1.9 gather_fusion.1
  238.1 6.8 %fusion.129 = f32[16,8,8,256]{3,1,2,0:T(8,128)} fusion(f32[16,8,8,256]{3,1,2,0:T(8,128)} %get-tuple-element.167, s32[]{:T(128)S(6)} %copy.98, bf16[8,8,7,256]{3,0,2,1:T(8,128)(2,1)S(1)} %bitcast.147, f32[8,7,256]{2,1,0:T(8,128)S(1)} %get-tuple-element.148, f32[8,256]{1,0:T(8,128)S(1)} %get-tuple-element.149, ...), kind=kOutput, calls=%fused_computation.6.clone.1 | convolution fusion | flops 99090432 | bytes 491524 | tf_op jit(solution)/shard_map/while/body/eval_jaxpr/gkpq,ngkq->ngp/dot_general | solution.py:44
  248.5 1.8 gather_fusion
  250.3 1.9 gather_fusion.1
  253.1 6.8 %fusion.129 = f32[16,8,8,256]{3,1,2,0:T(8,128)} fusion(f32[16,8,8,256]{3,1,2,0:T(8,128)} %get-tuple-element.167, s32[]{:T(128)S(6)} %copy.98, bf16[8,8,7,256]{3,0,2,1:T(8,128)(2,1)S(1)} %bitcast.147, f32[8,7,256]{2,1,0:T(8,128)S(1)} %get-tuple-element.148, f32[8,256]{1,0:T(8,128)S(1)} %get-tuple-element.149, ...), kind=kOutput, calls=%fused_computation.6.clone.1 | convolution fusion | flops 99090432 | bytes 491524 | tf_op jit(solution)/shard_map/while/body/eval_jaxpr/gkpq,ngkq->ngp/dot_general | solution.py:44
  265.3 1.9 gather_fusion.1
  268.1 6.8 %fusion.129 = f32[16,8,8,256]{3,1,2,0:T(8,128)} fusion(f32[16,8,8,256]{3,1,2,0:T(8,128)} %get-tuple-element.167, s32[]{:T(128)S(6)} %copy.98, bf16[8,8,7,256]{3,0,2,1:T(8,128)(2,1)S(1)} %bitcast.147, f32[8,7,256]{2,1,0:T(8,128)S(1)} %get-tuple-element.148, f32[8,256]{1,0:T(8,128)S(1)} %get-tuple-element.149, ...), kind=kOutput, calls=%fused_computation.6.clone.1 | convolution fusion | flops 99090432 | bytes 491524 | tf_op jit(solution)/shard_map/while/body/eval_jaxpr/gkpq,ngkq->ngp/dot_general | solution.py:44
  280.3 1.9 gather_fusion.1
  283.1 6.8 %fusion.129 = f32[16,8,8,256]{3,1,2,0:T(8,128)} fusion(f32[16,8,8,256]{3,1,2,0:T(8,128)} %get-tuple-element.167, s32[]{:T(128)S(6)} %copy.98, bf16[8,8,7,256]{3,0,2,1:T(8,128)(2,1)S(1)} %bitcast.147, f32[8,7,256]{2,1,0:T(8,128)S(1)} %get-tuple-element.148, f32[8,256]{1,0:T(8,128)S(1)} %get-tuple-element.149, ...), kind=kOutput, calls=%fused_computation.6.clone.1 | convolution fusion | flops 99090432 | bytes 491524 | tf_op jit(solution)/shard_map/while/body/eval_jaxpr/gkpq,ngkq->ngp/dot_general | solution.py:44
  295.3 1.9 gather_fusion.1
  298.1 6.8 %fusion.129 = f32[16,8,8,256]{3,1,2,0:T(8,128)} fusion(f32[16,8,8,256]{3,1,2,0:T(8,128)} %get-tuple-element.167, s32[]{:T(128)S(6)} %copy.98, bf16[8,8,7,256]{3,0,2,1:T(8,128)(2,1)S(1)} %bitcast.147, f32[8,7,256]{2,1,0:T(8,128)S(1)} %get-tuple-element.148, f32[8,256]{1,0:T(8,128)S(1)} %get-tuple-element.149, ...), kind=kOutput, calls=%fused_computation.6.clone.1 | convolution fusion | flops 99090432 | bytes 491524 | tf_op jit(solution)/shard_map/while/body/eval_jaxpr/gkpq,ngkq->ngp/dot_general | solution.py:44
  310.3 1.9 gather_fusion.1
  313.1 6.8 %fusion.129 = f32[16,8,8,256]{3,1,2,0:T(8,128)} fusion(f32[16,8,8,256]{3,1,2,0:T(8,128)} %get-tuple-element.167, s32[]{:T(128)S(6)} %copy.98, bf16[8,8,7,256]{3,0,2,1:T(8,128)(2,1)S(1)} %bitcast.147, f32[8,7,256]{2,1,0:T(8,128)S(1)} %get-tuple-element.148, f32[8,256]{1,0:T(8,128)S(1)} %get-tuple-element.149, ...), kind=kOutput, calls=%fused_computation.6.clone.1 | convolution fusion | flops 99090432 | bytes 491524 | tf_op jit(solution)/shard_map/while/body/eval_jaxpr/gkpq,ngkq->ngp/dot_general | solution.py:44
  325.3 1.9 gather_fusion.1
  328.1 6.8 %fusion.129 = f32[16,8,8,256]{3,1,2,0:T(8,128)} fusion(f32[16,8,8,256]{3,1,2,0:T(8,128)} %get-tuple-element.167, s32[]{:T(128)S(6)} %copy.98, bf16[8,8,7,256]{3,0,2,1:T(8,128)(2,1)S(1)} %bitcast.147, f32[8,7,256]{2,1,0:T(8,128)S(1)} %get-tuple-element.148, f32[8,256]{1,0:T(8,128)S(1)} %get-tuple-element.149, ...), kind=kOutput, calls=%fused_computation.6.clone.1 | convolution fusion | flops 99090432 | bytes 491524 | tf_op jit(solution)/shard_map/while/body/eval_jaxpr/gkpq,ngkq->ngp/dot_general | solution.py:44
  340.3 1.9 gather_fusion.1
  343.1 6.8 %fusion.129 = f32[16,8,8,256]{3,1,2,0:T(8,128)} fusion(f32[16,8,8,256]{3,1,2,0:T(8,128)} %get-tuple-element.167, s32[]{:T(128)S(6)} %copy.98, bf16[8,8,7,256]{3,0,2,1:T(8,128)(2,1)S(1)} %bitcast.147, f32[8,7,256]{2,1,0:T(8,128)S(1)} %get-tuple-element.148, f32[8,256]{1,0:T(8,128)S(1)} %get-tuple-element.149, ...), kind=kOutput, calls=%fused_computation.6.clone.1 | convolution fusion | flops 99090432 | bytes 491524 | tf_op jit(solution)/shard_map/while/body/eval_jaxpr/gkpq,ngkq->ngp/dot_general | solution.py:44
  355.3 1.9 gather_fusion.1
  358.0 6.8 %fusion.129 = f32[16,8,8,256]{3,1,2,0:T(8,128)} fusion(f32[16,8,8,256]{3,1,2,0:T(8,128)} %get-tuple-element.167, s32[]{:T(128)S(6)} %copy.98, bf16[8,8,7,256]{3,0,2,1:T(8,128)(2,1)S(1)} %bitcast.147, f32[8,7,256]{2,1,0:T(8,128)S(1)} %get-tuple-element.148, f32[8,256]{1,0:T(8,128)S(1)} %get-tuple-element.149, ...), kind=kOutput, calls=%fused_computation.6.clone.1 | convolution fusion | flops 99090432 | bytes 491524 | tf_op jit(solution)/shard_map/while/body/eval_jaxpr/gkpq,ngkq->ngp/dot_general | solution.py:44
  370.3 1.9 gather_fusion.1
  373.0 6.8 %fusion.129 = f32[16,8,8,256]{3,1,2,0:T(8,128)} fusion(f32[16,8,8,256]{3,1,2,0:T(8,128)} %get-tuple-element.167, s32[]{:T(128)S(6)} %copy.98, bf16[8,8,7,256]{3,0,2,1:T(8,128)(2,1)S(1)} %bitcast.147, f32[8,7,256]{2,1,0:T(8,128)S(1)} %get-tuple-element.148, f32[8,256]{1,0:T(8,128)S(1)} %get-tuple-element.149, ...), kind=kOutput, calls=%fused_computation.6.clone.1 | convolution fusion | flops 99090432 | bytes 491524 | tf_op jit(solution)/shard_map/while/body/eval_jaxpr/gkpq,ngkq->ngp/dot_general | solution.py:44
  385.3 1.9 gather_fusion.1
  388.0 6.8 %fusion.129 = f32[16,8,8,256]{3,1,2,0:T(8,128)} fusion(f32[16,8,8,256]{3,1,2,0:T(8,128)} %get-tuple-element.167, s32[]{:T(128)S(6)} %copy.98, bf16[8,8,7,256]{3,0,2,1:T(8,128)(2,1)S(1)} %bitcast.147, f32[8,7,256]{2,1,0:T(8,128)S(1)} %get-tuple-element.148, f32[8,256]{1,0:T(8,128)S(1)} %get-tuple-element.149, ...), kind=kOutput, calls=%fused_computation.6.clone.1 | convolution fusion | flops 99090432 | bytes 491524 | tf_op jit(solution)/shard_map/while/body/eval_jaxpr/gkpq,ngkq->ngp/dot_general | solution.py:44
  400.2 1.9 gather_fusion.1
  403.0 6.8 %fusion.129 = f32[16,8,8,256]{3,1,2,0:T(8,128)} fusion(f32[16,8,8,256]{3,1,2,0:T(8,128)} %get-tuple-element.167, s32[]{:T(128)S(6)} %copy.98, bf16[8,8,7,256]{3,0,2,1:T(8,128)(2,1)S(1)} %bitcast.147, f32[8,7,256]{2,1,0:T(8,128)S(1)} %get-tuple-element.148, f32[8,256]{1,0:T(8,128)S(1)} %get-tuple-element.149, ...), kind=kOutput, calls=%fused_computation.6.clone.1 | convolution fusion | flops 99090432 | bytes 491524 | tf_op jit(solution)/shard_map/while/body/eval_jaxpr/gkpq,ngkq->ngp/dot_general | solution.py:44
  413.4 9.7 %fusion.78 = f32[128,6,8,64]{3,2,1,0:T(8,128)S(1)} fusion(bf16[128,6,8,64]{3,2,1,0:T(8,128)(2,1)} %copy.54, bf16[128,64,6,64]{3,1,2,0:T(8,128)(2,1)} %copy.55), kind=kOutput, calls=%fused_computation.130 | convolution fusion | flops 50331648 | bytes 8650752 | tf_op jit(solution)/shard_map/pasb,psnb->psna/dot_general | solution.py:130
  423.1 3.1 fusion.21
  426.5 5.8 %fusion.11 = f32[8,128,256]{2,0,1:T(8,128)} fusion(f32[8,128,256]{2,0,1:T(8,128)} %bitcast.152, bf16[128,64,256]{2,1,0:T(8,128)(2,1)} %param.15, f32[128,8,64]{2,1,0:T(8,128)S(1)} %copy.57, bf16[8,64,1]{1,0,2:T(8,128)(2,1)S(1)} %fusion.33, bf16[64,128,64]{2,1,0:T(8,128)(2,1)S(1)} %reshape.100), kind=kOutput, calls=%fused_computation.52 | convolution fusion | flops 42336256 | bytes 7603200 | tf_op jit(solution)/shard_map/lbp,lnb->nlp/dot_general | solution.py:144
  (250 shorter events, 81.8 us)
Async XLA Ops:
  2.1 165.8 %collective-permute-start.8 = (bf16[8,16384]{1,0:T(8,128)(2,1)}, bf16[8,16384]{1,0:T(8,128)(2,1)}, u32[]{:S(2)}, u32[]{:S(2)}) collective-permute-start(bf16[8,16384]{1,0:T(8,128)(2,1)} %get-tuple-element.98), channel_id=1, source_target_pairs={{1,0},{2,1},{3,2},{4,3},{5,4},{6,5},{7,6},{8,7},{9,8},{10,9},{11,1... | collective-permute-start | bytes 786440 | tf_op jit(solution)/shard_map/ppermute | solution.py:24
  4.5 163.4 %collective-permute-start.7 = (bf16[8,16384]{1,0:T(8,128)(2,1)}, bf16[8,16384]{1,0:T(8,128)(2,1)}, u32[]{:S(2)}, u32[]{:S(2)}) collective-permute-start(bf16[8,16384]{1,0:T(8,128)(2,1)} %get-tuple-element.97), channel_id=1, source_target_pairs={{0,1},{1,2},{2,3},{3,4},{4,5},{5,6},{6,7},{7,8},{8,9},{9,10},{10,1... | collective-permute-start | bytes 786440 | tf_op jit(solution)/shard_map/ppermute | solution.py:24
  9.9 155.7 %collective-permute-start.10 = (f32[3,16384]{1,0:T(4,128)}, f32[3,16384]{1,0:T(4,128)}, u32[]{:S(2)}, u32[]{:S(2)}) collective-permute-start(f32[3,16384]{1,0:T(4,128)} %get-tuple-element.96), channel_id=1, source_target_pairs={{1,0},{2,1},{3,2},{4,3},{5,4},{6,5},{7,6},{8,7},{9,8},{10,9},{11,1... | collective-permute-start | bytes 589832 | tf_op jit(solution)/shard_map/ppermute | solution.py:24
  12.3 153.3 %collective-permute-start.9 = (f32[3,16384]{1,0:T(4,128)}, f32[3,16384]{1,0:T(4,128)}, u32[]{:S(2)}, u32[]{:S(2)}) collective-permute-start(f32[3,16384]{1,0:T(4,128)} %get-tuple-element.95), channel_id=1, source_target_pairs={{0,1},{1,2},{2,3},{3,4},{4,5},{5,6},{6,7},{7,8},{8,9},{9,10},{10,1... | collective-permute-start | bytes 589832 | tf_op jit(solution)/shard_map/ppermute | solution.py:24
  20.3 9.9 %copy-start.15 = (s32[1,128,6]{1,0,2:T(1,128)S(1)}, s32[1,128,6]{1,0,2:T(1,128)}, u32[]{:S(2)}) copy-start(s32[1,128,6]{1,0,2:T(1,128)} %param.21) | copy-start | bytes 9220
  20.3 10.1 %copy-start.16 = (s32[1,128]{1,0:T(1,128)S(1)}, s32[1,128]{1,0:T(1,128)}, u32[]{:S(2)}) copy-start(s32[1,128]{1,0:T(1,128)} %param.22) | copy-start | bytes 1540
  26.0 50.3 %collective-permute-start = (f32[8,64]{1,0:T(8,128)S(1)}, f32[8,64]{1,0:T(8,128)S(1)}, u32[]{:S(2)}, u32[]{:S(2)}) collective-permute-start(f32[8,64]{1,0:T(8,128)S(1)} %fusion.29), channel_id=1, source_target_pairs={{0,1},{1,0},{2,3},{3,2},{4,5},{5,4},{6,7},{7,6},{8,9},{9,8},{10,11... | collective-permute-start | bytes 6152 | tf_op jit(solution)/shard_map/ppermute | solution.py:18
  70.6 5.7 %copy-start.11 = (f32[64,64]{1,0:T(8,128)S(1)}, f32[64,64]{1,0:T(8,128)}, u32[]{:S(2)}) copy-start(f32[64,64]{1,0:T(8,128)} %get-tuple-element.74) | copy-start | bytes 49156
  70.6 5.8 %copy-start.12 = (f32[64,64]{1,0:T(8,128)S(1)}, f32[64,64]{1,0:T(8,128)}, u32[]{:S(2)}) copy-start(f32[64,64]{1,0:T(8,128)} %dynamic-slice_reduce_fusion.24) | copy-start | bytes 49156
  74.0 18.8 %copy-start.10 = (f32[64,64]{1,0:T(8,128)S(1)}, f32[64,64]{1,0:T(8,128)}, u32[]{:S(2)}) copy-start(f32[64,64]{1,0:T(8,128)} %get-tuple-element.72) | copy-start | bytes 49156
  76.6 16.2 %collective-permute-start.1 = (f32[8,64]{1,0:T(8,128)S(1)}, f32[8,64]{1,0:T(8,128)S(1)}, u32[]{:S(2)}, u32[]{:S(2)}) collective-permute-start(f32[8,64]{1,0:T(8,128)S(1)} %convolution_add_fusion.11), channel_id=1, source_target_pairs={{0,2},{1,3},{2,0},{3,1},{4,6},{5,7},{6,4},{7,5},{8,10},{9,11},{10,... | collective-permute-start | bytes 6152 | tf_op jit(solution)/shard_map/ppermute | solution.py:18
  79.0 330.8 %all-to-all-start = ((bf16[128,6,512]{2,1,0:T(8,128)(2,1)}), bf16[128,6,512]{2,1,0:T(8,128)(2,1)}, u32[]{:S(2)}, u32[]{:S(2)}) async-start(bf16[128,6,512]{2,1,0:T(8,128)(2,1)} %broadcast_select_fusion), calls=%async_computation | async-start | bytes 2097152 | tf_op jit(solution)/shard_map/all_to_all | solution.py:92
  93.0 12.4 %collective-permute-start.2 = (f32[8,64]{1,0:T(8,128)S(1)}, f32[8,64]{1,0:T(8,128)S(1)}, u32[]{:S(2)}, u32[]{:S(2)}) collective-permute-start(f32[8,64]{1,0:T(8,128)S(1)} %convolution_add_fusion.9), channel_id=1, source_target_pairs={{0,4},{1,5},{2,6},{3,7},{4,0},{5,1},{6,2},{7,3},{8,12},{9,13},{10,... | collective-permute-start | bytes 6152 | tf_op jit(solution)/shard_map/ppermute | solution.py:18
  105.7 16.9 %collective-permute-start.3 = (f32[8,64]{1,0:T(8,128)S(1)}, f32[8,64]{1,0:T(8,128)S(1)}, u32[]{:S(2)}, u32[]{:S(2)}) collective-permute-start(f32[8,64]{1,0:T(8,128)S(1)} %convolution_add_fusion.7), channel_id=1, source_target_pairs={{0,8},{1,9},{2,10},{3,11},{4,12},{5,13},{6,14},{7,15},{8,0},{9,1},... | collective-permute-start | bytes 6152 | tf_op jit(solution)/shard_map/ppermute | solution.py:18
  108.4 15.0 %copy-start.4 = (f32[64,64]{1,0:T(8,128)S(1)}, f32[64,64]{1,0:T(8,128)}, u32[]{:S(2)}) copy-start(f32[64,64]{1,0:T(8,128)} %get-tuple-element.69) | copy-start | bytes 49156
  108.4 16.3 %copy-start.3 = (f32[64,64]{1,0:T(8,128)S(1)}, f32[64,64]{1,0:T(8,128)}, u32[]{:S(2)}) copy-start(f32[64,64]{1,0:T(8,128)} %get-tuple-element.66) | copy-start | bytes 49156
  108.4 16.5 %copy-start.2 = (f32[64,64]{1,0:T(8,128)S(1)}, f32[64,64]{1,0:T(8,128)}, u32[]{:S(2)}) copy-start(f32[64,64]{1,0:T(8,128)} %get-tuple-element.67) | copy-start | bytes 49156
  108.4 18.4 %copy-start.13 = (s32[128,6]{0,1:T(8,128)S(1)}, s32[128,6]{0,1:T(8,128)}, u32[]{:S(2)}) copy-start(s32[128,6]{0,1:T(8,128)} %param.20) | copy-start | bytes 9220
  108.4 20.2 %copy-start.1 = (f32[64,64]{1,0:T(8,128)S(1)}, f32[64,64]{1,0:T(8,128)}, u32[]{:S(2)}) copy-start(f32[64,64]{1,0:T(8,128)} %get-tuple-element.64) | copy-start | bytes 49156
  108.5 24.6 %copy-start = (f32[3,32768]{1,0:T(4,128)S(1)}, f32[3,32768]{1,0:T(4,128)}, u32[]{:S(2)}) copy-start(f32[3,32768]{1,0:T(4,128)} %param.13) | copy-start | bytes 1179652
  123.6 1.2 collective-permute-start.4
  125.0 3.6 collective-permute-start.5
  128.9 32.9 %collective-permute-start.6 = (f32[8,64]{1,0:T(8,128)S(1)}, f32[8,64]{1,0:T(8,128)S(1)}, u32[]{:S(2)}, u32[]{:S(2)}) collective-permute-start(f32[8,64]{1,0:T(8,128)S(1)} %convolution_add_fusion.1), channel_id=1, source_target_pairs={{0,64},{16,80},{32,96},{48,112},{64,0},{80,16},{96,32},{112,48},{1... | collective-permute-start | bytes 6152 | tf_op jit(solution)/shard_map/ppermute | solution.py:18
  143.1 18.7 %copy-start.14 = (s32[1,128,6]{1,0,2:T(1,128)S(1)}, s32[1,128,6]{1,0,2:T(1,128)}, u32[]{:S(2)}) copy-start(s32[1,128,6]{1,0,2:T(1,128)} %param.23) | copy-start | bytes 9220
  143.1 20.9 %copy-start.9 = (f32[64,64]{1,0:T(8,128)S(1)}, f32[64,64]{1,0:T(8,128)}, u32[]{:S(2)}) copy-start(f32[64,64]{1,0:T(8,128)} %get-tuple-element.53) | copy-start | bytes 49156
  143.1 21.2 %copy-start.8 = (f32[64,64]{1,0:T(8,128)S(1)}, f32[64,64]{1,0:T(8,128)}, u32[]{:S(2)}) copy-start(f32[64,64]{1,0:T(8,128)} %get-tuple-element.54) | copy-start | bytes 49156
  143.1 21.6 %copy-start.7 = (f32[64,64]{1,0:T(8,128)S(1)}, f32[64,64]{1,0:T(8,128)}, u32[]{:S(2)}) copy-start(f32[64,64]{1,0:T(8,128)} %get-tuple-element.55) | copy-start | bytes 49156
  143.1 21.9 %copy-start.6 = (f32[64,64]{1,0:T(8,128)S(1)}, f32[64,64]{1,0:T(8,128)}, u32[]{:S(2)}) copy-start(f32[64,64]{1,0:T(8,128)} %get-tuple-element.56) | copy-start | bytes 49156
  143.1 22.3 %copy-start.5 = (f32[64,64]{1,0:T(8,128)S(1)}, f32[64,64]{1,0:T(8,128)}, u32[]{:S(2)}) copy-start(f32[64,64]{1,0:T(8,128)} %get-tuple-element.50) | copy-start | bytes 49156
where the time goes:
time: 441 us; the launch traced here: 432 us
  local copies, waits for them, and re-layouts  202 us (46%)
  matrix products  140 us (32%)
  starting transfers between devices  40.3 us (9%)
  loops' own time  32.8 us (7%)
  other arithmetic  8.98 us (2%)
  waiting for transfers between devices  8.17 us (2%)
    dot_general x16, matrix products, one_group(): jnp.einsum('gkpq,ngkq->ngp', kernel, source_values, preferred_element_typ...  109 us
    another operation x1, loops' own time, near_field(): blocks = lax.map(one_group, starts)  32.8 us
    gather x32, local copies, waits for them, and re-layouts, one_group(): source_points = seen_points[:, picked]  31.4 us
    dynamic_slice x1, local copies, waits for them, and re-layouts, shards(): transfer_table[node_index]  30.3 us
    gather x16, local copies, waits for them, and re-layouts, one_group(): source_values = seen_values[:, picked]  29 us
    unnamed x39, local copies, waits for them, and re-layouts  21.9 us
    dynamic_slice x16, local copies, waits for them, and re-layouts, near_field(): blocks = lax.map(one_group, starts)  20.4 us
    another operation x1, local copies, waits for them, and re-layouts, shards(): coupling_blocks = far_coupling[0].reshape(owners, rank, slot_count, rank)  18.7 us
  transfers between devices with their start and end apart: 12, of which 3 were waited for; matrix products, arithmetic and copies ran while one was open for 75% of the time, Pallas kernels for 0%

commit v1 on v0

v1 whole, which is shorter than its diff:
```python
import functools
import math

import jax
import jax.numpy as jnp
from jax import lax
from jax.experimental import pallas as pl
from jax.experimental.pallas import tpu as pltpu
from jax.sharding import PartitionSpec as P

LEAF = 256
R = 64
N = 8
EDGE = 64
OWN = 128
SEEN = 256
SLOTS = 6
NEAR = 6
FEAT = 48
F32 = jnp.float32
BF16 = jnp.bfloat16

kernel_scale = 0.25 / (4.0 * math.pi)
smoothing = 0.0025
inverse_scale = 1.0 / kernel_scale

NN = (((1,), (0,)), ((), ()))
NT = (((1,), (1,)), ((), ()))
VMEM = pl.BlockSpec(memory_space=pltpu.VMEM)
SMEM = pl.BlockSpec(memory_space=pltpu.SMEM)
ANY = pl.BlockSpec(memory_space=pl.ANY)


def dot(a, b, dims=NN):
    return lax.dot_general(a, b, dims, preferred_element_type=F32)


def exact_dot(a, b, dims=NN):
    return lax.dot_general(a, b, dims, precision=lax.Precision.HIGHEST, preferred_element_type=F32)


def aligned(index, size):
    return pl.ds(pl.multiple_of(index * size, size), size)


def params(megabytes):
    return pltpu.CompilerParams(vmem_limit_bytes=megabytes << 20)


def round16(x):
    return x.astype(BF16).astype(F32)


def features(points, is_target):
    width = points.shape[1]
    row = lax.broadcasted_iota(jnp.int32, (8, width), 0)
    padded = jnp.concatenate([points, jnp.ones((5, width), F32)], 0)
    x = jnp.where(row < 3, (padded - 1.0) * inverse_scale, 0.0)
    high = round16(x)
    low = round16(x - high)
    x = high + low
    square = jnp.broadcast_to(jnp.sum(x * x, axis=0, keepdims=True), (8, width))
    if is_target:
        square = square + smoothing * inverse_scale * inverse_scale
    s0 = round16(square)
    s1 = round16(square - s0)
    s2 = square - s0 - s1
    zero = jnp.zeros_like(x)
    if is_target:
        last = jnp.where(row == 0, s0, jnp.where(row == 1, s1, jnp.where(row == 2, s2, jnp.where(row < 6, 1.0, 0.0))))
        parts = [-2.0 * high, -2.0 * high, -2.0 * low, -2.0 * low, last, zero]
    else:
        last = jnp.where(row < 3, 1.0, jnp.where(row == 3, s0, jnp.where(row == 4, s1, jnp.where(row == 5, s2, 0.0))))
        parts = [high, low, high, low, last, zero]
    return jnp.concatenate(parts, 0)


def inverse_root(distance):
    return lax.rsqrt(distance.astype(BF16))


def moment_kernel(send_leaf, send_count, values, basis, transfer, message, device_moment, moments):
    def four_leaves(g, total):
        picked = []
        for j in range(4):
            leaf = g * 4 + j
            v = values[:, aligned(leaf, LEAF)].astype(BF16)
            m = round16(dot(v, basis[leaf], NT))
            moments[leaf] = jnp.concatenate([m, m], 1)
            picked.append(m)
        return total + dot(jnp.concatenate(picked, 0).astype(BF16), transfer[:, aligned(g, 4 * R)])

    total = lax.fori_loop(0, OWN // 4, four_leaves, jnp.zeros((4 * N, 4 * R), F32))
    moment = total[0:N, 0:R]
    for j in range(1, 4):
        moment = moment + total[j * N : (j + 1) * N, j * R : (j + 1) * R]
    device_moment[...] = moment * (1.0 / math.sqrt(OWN))

    is_left = lax.broadcasted_iota(jnp.int32, (N, 2 * R), 1) < R

    def two_receivers(g, carry):
        rows = []
        for j in range(2):
            p = g * 2 + j
            count = send_count[0, p]
            for pair in range(SLOTS // 2):
                left = moments[send_leaf[2 * pair, p]]
                right = moments[send_leaf[2 * pair + 1, p]]
                left = jnp.where(2 * pair < count, left, 0.0)
                right = jnp.where(2 * pair + 1 < count, right, 0.0)
                rows.append(jnp.where(is_left, left, right))
        message[aligned(g, 48), :] = jnp.concatenate(rows, 0).astype(BF16)
        return carry

    lax.fori_loop(0, OWN // 2, two_receivers, 0, unroll=2)


def self_kernel(points, values, out):
    def four_leaves(g, carry):
        kernels = []
        for j in range(4):
            x = points[:, aligned(g * 4 + j, LEAF)]
            target = features(x, True).astype(BF16)
            source = features(x, False).T.astype(BF16)
            kernels.append(inverse_root(dot(source, target)))
        for j in range(4):
            v = values[:, aligned(g * 4 + j, LEAF)].astype(BF16)
            out[:, aligned(g * 4 + j, LEAF)] = dot(v, kernels[j])
        return carry

    lax.fori_loop(0, OWN // 4, four_leaves, 0)


def near_kernel(
    near_list, points_below, points, points_above, values_below, values, values_above, before, out,
    sources, targets, seen_values,
):
    def stage(point_ref, value_ref, first, count, own):
        def one(i, carry):
            x = point_ref[:, aligned(i, LEAF)]
            sources[first + i] = features(x, False).T.astype(BF16)
            seen_values[first + i] = value_ref[:, aligned(i, LEAF)]
            if own:
                targets[i] = features(x, True).astype(BF16)
            return carry

        lax.fori_loop(0, count, one, 0, unroll=2)

    stage(points_below, values_below, 0, EDGE, False)
    stage(points, values, EDGE, OWN, True)
    stage(points_above, values_above, EDGE + OWN, EDGE, False)

    def two_leaves(g, carry):
        for j in range(2):
            leaf = g * 2 + j
            target = targets[leaf]
            seen = [near_list[k, leaf] for k in range(NEAR)]
            kernels = [inverse_root(dot(sources[e], target)) for e in seen]
            total = before[:, aligned(leaf, LEAF)]
            for k in range(NEAR):
                total = total + dot(seen_values[seen[k]].astype(BF16), kernels[k])
            out[:, aligned(leaf, LEAF)] = total
        return carry

    lax.fori_loop(0, OWN // 2, two_leaves, 0)


def fetch(table, row, matrices, slot):
    flat = table[pl.ds(row, 1), :]
    for j in range(R // 2):
        pair = flat[:, j * 2 * R : (j + 1) * 2 * R]
        matrices[slot, 2 * j : 2 * j + 1, 0:R] = pair[:, 0:R]
        matrices[slot, 2 * j + 1 : 2 * j + 2, 0:R] = pair[:, R : 2 * R]


def upward(ups, matrices, slot):
    result = []
    for c in range(0, len(ups), 2):
        left = exact_dot(ups[c], matrices[slot + c])
        result.append(left + exact_dot(ups[c + 1], matrices[slot + c + 1]))
    return result


def group_tree_kernel(place, gathered, table, siblings, group_moment, matrices, levels_ref):
    group = place[0]
    dev = place[1]
    slot = 0
    ups = [gathered[c * N : (c + 1) * N, :] for c in range(16)]
    first = [0]
    for level in range(4):
        count = 16 >> level
        base = 2 * OWN - 2 * (OWN >> level)

        def fill(i, carry):
            fetch(table, base + group * count + i, matrices, slot + i)
            return carry

        lax.fori_loop(0, count, fill, 0)
        slot += count
    slot = 0
    for level in range(4):
        count = 16 >> level
        for c in range(count):
            levels_ref[slot + c] = ups[c]
        siblings[level] = levels_ref[slot + ((dev >> level) ^ 1)]
        ups = upward(ups, matrices, slot)
        slot += count
    group_moment[...] = ups[0]


def far_kernel(
    place, far_target, incoming, siblings, group_moments, near,
    coupling_hbm, transfer_hbm, basis_hbm, top_transfer_hbm, top_coupling_hbm,
    out,
    coupling, transfer, basis, top_transfer, top_coupling, far_local, matrices, levels_ref, sems,
):
    chunks = 4
    chunk = OWN // chunks
    copies = []
    for i in range(chunks):
        copies.append(pltpu.make_async_copy(coupling_hbm.at[pl.ds(i * chunk, chunk)], coupling.at[pl.ds(i * chunk, chunk)], sems.at[i]))
    rest = [(top_transfer_hbm, top_transfer), (top_coupling_hbm, top_coupling), (transfer_hbm, transfer), (basis_hbm, basis)]
    for i, (source, target) in enumerate(rest):
        copies.append(pltpu.make_async_copy(source, target, sems.at[chunks + i]))
    for copy in copies:
        copy.start()

    far_local[...] = jnp.zeros_like(far_local)
    is_left = lax.broadcasted_iota(jnp.int32, (N, 2 * R), 1) < R

    for i in range(chunks):
        copies[i].wait()

        def two_senders(g, carry):
            arrived = incoming[aligned(g, 48), :].astype(F32)
            results = []
            for j in range(2):
                p = g * 2 + j
                for pair in range(SLOTS // 2):
                    tile = arrived[(j * 3 + pair) * N : (j * 3 + pair + 1) * N, :]
                    left = jnp.where(is_left, tile, 0.0)
                    right = jnp.where(is_left, 0.0, tile)
                    both = jnp.concatenate([left, right], 0).astype(BF16)
                    matrix = coupling[p, :, pair * 2 * R : (pair + 1) * 2 * R]
                    results.append(dot(both, matrix, NT))
            for j in range(2):
                p = g * 2 + j
                for slot in range(SLOTS):
                    leaf = far_target[slot, p]
                    part = results[j * 3 + slot // 2][(slot % 2) * N : (slot % 2 + 1) * N, :]
                    far_local[leaf] = far_local[leaf] + part
            return carry

        lax.fori_loop(i * chunk // 2, (i + 1) * chunk // 2, two_senders, 0, unroll=2)

    group = place[0]
    owner = group * 16 + place[1]
    copies[chunks].wait()
    copies[chunks + 1].wait()

    def fill_top(i, carry):
        fetch(top_transfer, 240 + i, matrices, i)
        return carry

    lax.fori_loop(0, 12, fill_top, 0)
    for level in range(7):
        node = 2 * OWN - 2 * (OWN >> level) + (owner >> level)
        fetch(top_coupling, node, matrices, 12 + level)
        if level < 6:
            fetch(top_transfer, node, matrices, 19 + level)
    sibling_moments = [siblings[level] for level in range(4)]
    ups = [group_moments[c * N : (c + 1) * N, :] for c in range(8)]
    slot = 0
    for level in range(3):
        count = 8 >> level
        for c in range(count):
            levels_ref[slot + c] = ups[c]
        sibling_moments.append(levels_ref[slot + ((group >> level) ^ 1)])
        if level < 2:
            ups = upward(ups, matrices, slot)
        slot += count
    field = exact_dot(sibling_moments[6], matrices[12 + 6], NT)
    for level in reversed(range(6)):
        coupled = exact_dot(sibling_moments[level], matrices[12 + level], NT)
        field = coupled + exact_dot(field, matrices[19 + level], NT)
    field = round16(field)

    wide = jnp.concatenate([jnp.concatenate([field] * 4, 1)] * 4, 0)
    row_leaf = lax.broadcasted_iota(jnp.int32, (4 * N, 4 * R), 0) // N
    column_leaf = lax.broadcasted_iota(jnp.int32, (4 * N, 4 * R), 1) // R
    fields = jnp.where(row_leaf == column_leaf, wide, 0.0).astype(BF16)
    copies[chunks + 2].wait()
    copies[chunks + 3].wait()

    def four_leaves(g, carry):
        local = dot(fields, transfer[:, aligned(g, 4 * R)], NT)
        for j in range(4):
            leaf = g * 4 + j
            total = (local[j * N : (j + 1) * N, :] + far_local[leaf]).astype(BF16)
            out[:, aligned(leaf, LEAF)] = near[:, aligned(leaf, LEAF)] + dot(total, basis[leaf])
        return carry

    lax.fori_loop(0, OWN // 4, four_leaves, 0, unroll=2)


def from_behind(block, axis, distance):
    devices = range(lax.axis_size(axis))
    route = [(i - distance, i) for i in devices if i - distance in devices]
    return lax.ppermute(block, axis, route)


def shards(
    positions, right_sides, leaf_basis, leaf_transfer, far_coupling, top_transfer, top_coupling,
    near_list, send_leaf, send_count, far_target,
):
    both = ("group", "dev")
    points = OWN * LEAF
    rim = EDGE * LEAF
    place = jnp.stack([lax.axis_index("group"), lax.axis_index("dev")]).astype(jnp.int32)
    rounded = right_sides.astype(BF16)
    values_below = from_behind(rounded[:, points - rim :], both, 1)
    values_above = from_behind(rounded[:, :rim], both, -1)
    points_below = from_behind(positions[:, points - rim :], both, 1)
    points_above = from_behind(positions[:, :rim], both, -1)

    message, device_moment = pl.pallas_call(
        moment_kernel,
        out_shape=(jax.ShapeDtypeStruct((OWN * 24, 2 * R), BF16), jax.ShapeDtypeStruct((N, R), F32)),
        in_specs=[SMEM, SMEM, VMEM, VMEM, VMEM],
        out_specs=(VMEM, VMEM),
        scratch_shapes=[pltpu.VMEM((OWN, N, 2 * R), F32)],
        compiler_params=params(32),
        cost_estimate=pl.CostEstimate(flops=10**9, bytes_accessed=8 << 20, transcendentals=0),
        name="moments",
    )(send_leaf[0].T, send_count, right_sides, leaf_basis, leaf_transfer)

    gathered = lax.all_gather(device_moment, "dev", axis=0, tiled=True)
    incoming = lax.all_to_all(message, both, split_axis=0, concat_axis=0, tiled=True)

    near_self = pl.pallas_call(
        self_kernel,
        out_shape=jax.ShapeDtypeStruct((N, points), F32),
        in_specs=[VMEM, VMEM],
        out_specs=VMEM,
        compiler_params=params(32),
        cost_estimate=pl.CostEstimate(flops=8 * 10**9, bytes_accessed=3 << 20, transcendentals=0),
        name="near_self",
    )(positions, right_sides)

    gathered, near_self = lax.optimization_barrier((gathered, near_self))
    siblings, group_moment = pl.pallas_call(
        group_tree_kernel,
        out_shape=(jax.ShapeDtypeStruct((4, N, R), F32), jax.ShapeDtypeStruct((N, R), F32)),
        in_specs=[SMEM, VMEM, VMEM],
        out_specs=(VMEM, VMEM),
        scratch_shapes=[pltpu.VMEM((30, R, R), F32), pltpu.VMEM((30, N, R), F32)],
        compiler_params=params(32),
        cost_estimate=pl.CostEstimate(flops=10**8, bytes_accessed=4 << 20, transcendentals=0),
        name="group_tree",
    )(place, gathered, top_transfer)
    group_moments = lax.all_gather(group_moment, "group", axis=0, tiled=True)
    near_self, siblings = lax.optimization_barrier((near_self, siblings))

    near = pl.pallas_call(
        near_kernel,
        out_shape=jax.ShapeDtypeStruct((N, points), F32),
        in_specs=[SMEM] + [VMEM] * 7,
        out_specs=VMEM,
        scratch_shapes=[
            pltpu.VMEM((SEEN, LEAF, FEAT), BF16),
            pltpu.VMEM((OWN, FEAT, LEAF), BF16),
            pltpu.VMEM((SEEN, N, LEAF), F32),
        ],
        compiler_params=params(56),
        cost_estimate=pl.CostEstimate(flops=60 * 10**9, bytes_accessed=6 << 20, transcendentals=0),
        name="near_listed",
    )(
        near_list.T, points_below, positions, points_above,
        values_below.astype(F32), right_sides, values_above.astype(F32), near_self,
    )

    return pl.pallas_call(
        far_kernel,
        out_shape=jax.ShapeDtypeStruct((N, points), F32),
        in_specs=[SMEM, SMEM, VMEM, VMEM, VMEM, VMEM, ANY, ANY, ANY, ANY, ANY],
        out_specs=VMEM,
        scratch_shapes=[
            pltpu.VMEM((OWN, R, SLOTS * R), BF16),
            pltpu.VMEM((R, OWN * R), BF16),
            pltpu.VMEM((OWN, R, LEAF), BF16),
            pltpu.VMEM((254, R * R), F32),
            pltpu.VMEM((254, R * R), F32),
            pltpu.VMEM((OWN, N, R), F32),
            pltpu.VMEM((25, R, R), F32),
            pltpu.VMEM((14, N, R), F32),
            pltpu.SemaphoreType.DMA((8,)),
        ],
        compiler_params=params(56),
        cost_estimate=pl.CostEstimate(flops=2 * 10**9, bytes_accessed=22 << 20, transcendentals=0),
        name="far_field",
    )(
        place, far_target[0].T, incoming, siblings, group_moments, near,
        far_coupling[0], leaf_transfer, leaf_basis, top_transfer, top_coupling,
    )


def solution(mesh):
    both = ("group", "dev")
    placed = (
        P(None, both), P(None, both), P(both, None, None), P(None, both), P(both, None, None, None),
        P(), P(), P(both, None), P(both, None, None), P(both, None), P(both, None, None),
    )
    return jax.shard_map(shards, mesh=mesh, in_specs=placed, out_specs=P(None, both), check_vma=False)
```

time: 441 us -> 211 us (0.48); the launches traced: 432 us -> 207 us
  local copies, waits for them, and re-layouts: 202 us -> 11.5 us
  matrix products: 140 us -> 0 us
  Pallas kernels: 0 us -> 131 us
  blocking collectives: 0 us -> 36.7 us
  loops' own time: 32.8 us -> 0 us
  starting transfers between devices: 40.3 us -> 24.9 us
  waiting for transfers between devices: 8.17 us -> 0.01 us
  other arithmetic: 8.98 us -> 3.17 us
    dot_general x47 -> x0, matrix products: 140 us -> none  [the longest x16 109 us: one_group(): jnp.einsum('gkpq,ngkq->ngp', kernel, source_values, preferred_element_typ...]
    pallas_call x0 -> x5, Pallas kernels: none -> 131 us  [the longest x1 77.3 us: shards(): pl.pallas_call(near_kernel, out_shape=jax.ShapeDtypeStruct((N, points), F...]
    dynamic_slice x51 -> x0, local copies, waits for them, and re-layouts: 70.7 us -> none  [the longest x1 30.3 us: shards(): transfer_table[node_index]]
    gather x50 -> x0, local copies, waits for them, and re-layouts: 66.1 us -> none  [the longest x32 31.4 us: one_group(): source_points = seen_points[:, picked]]
    all_gather x0 -> x2, blocking collectives: none -> 36.7 us  [the longest x1 22.2 us: shards(): gathered = lax.all_gather(device_moment, 'dev', axis=0, tiled=True)]
    another operation x1 -> x0, loops' own time: 32.8 us -> none  [near_field(): blocks = lax.map(one_group, starts)]
    another operation x1 -> x0, local copies, waits for them, and re-layouts: 18.7 us -> none  [shards(): coupling_blocks = far_coupling[0].reshape(owners, rank, slot_count, rank)]
    ppermute x7 -> x0, starting transfers between devices: 13.6 us -> none  [partner(): return lax.ppermute(value, axis, pairs)]
  transfers between devices with their start and end apart: 12 -> 5, of which waited for: 3 -> 0; matrix products, arithmetic and copies ran while one was open for 75% -> 2% of each run, Pallas kernels for 0% -> 53%
where the time goes in v1:
time: 211 us; the launch traced here: 207 us
  Pallas kernels  131 us (62%)
  blocking collectives  36.7 us (17%)
  starting transfers between devices  24.9 us (12%)
  local copies, waits for them, and re-layouts  11.5 us (5%)
  other arithmetic  3.17 us (2%)
    pallas_call x1, Pallas kernels, shards(): pl.pallas_call(near_kernel, out_shape=jax.ShapeDtypeStruct((N, points), F...  77.3 us
    all_gather x1, blocking collectives, shards(): gathered = lax.all_gather(device_moment, 'dev', axis=0, tiled=True)  22.2 us
    pallas_call x1, Pallas kernels, shards(): pl.pallas_call(far_kernel, out_shape=jax.ShapeDtypeStruct((N, points), F3...  21.6 us
    pallas_call x1, Pallas kernels, shards(): pl.pallas_call(self_kernel, out_shape=jax.ShapeDtypeStruct((N, points), F...  15.8 us
    all_gather x1, blocking collectives, shards(): group_moments = lax.all_gather(group_moment, 'group', axis=0, tiled=True)  14.4 us
    all_to_all x1, starting transfers between devices, shards(): lax.all_to_all(message, both, split_axis=0, concat_axis=0, tiled=True)  13.3 us
    pallas_call x1, Pallas kernels, shards(): pl.pallas_call(moment_kernel, out_shape=(jax.ShapeDtypeStruct((OWN * 24,...  12 us
    ppermute x4, starting transfers between devices, from_behind(): return lax.ppermute(block, axis, route)  11.7 us
  transfers between devices with their start and end apart: 5, of which 0 were waited for; matrix products, arithmetic and copies ran while one was open for 2% of the time, Pallas kernels for 53%

profile of v1, /device:TPU:4, one launch (start us, length us, event | category | flops | bytes accessed | tf_op | source)
XLA Modules:
  0.0 207.3 jit_solution(6583432789325132292)
XLA Ops:
  0.0 0.0 copy-start.3
  0.0 0.0 copy-start.2
  0.0 1.4 convert_element_type.9
  1.4 0.7 fusion
  2.2 3.1 %collective-permute-start.2 = (bf16[8,16384]{1,0:T(8,128)(2,1)}, bf16[8,16384]{1,0:T(8,128)(2,1)S(1)}, u32[]{:S(2)}, u32[]{:S(2)}) collective-permute-start(bf16[8,16384]{1,0:T(8,128)(2,1)} %get-tuple-element.22), channel_id=1, source_target_pairs={{0,1},{1,2},{2,3},{3,4},{4,5},{5,6},{6,7},{7,8},{8,9},{9,10},{10,1... | collective-permute-start | bytes 786440 | tf_op jit(solution)/shard_map/ppermute | solution.py:309
  5.3 2.7 %collective-permute-start.3 = (bf16[8,16384]{1,0:T(8,128)(2,1)S(1)}, bf16[8,16384]{1,0:T(8,128)(2,1)S(1)}, u32[]{:S(2)}, u32[]{:S(2)}) collective-permute-start(bf16[8,16384]{1,0:T(8,128)(2,1)S(1)} %get-tuple-element.21), channel_id=1, source_target_pairs={{1,0},{2,1},{3,2},{4,3},{5,4},{6,5},{7,6},{8,7},{9,8},{10,9},{11,1... | collective-permute-start | bytes 786440 | tf_op jit(solution)/shard_map/ppermute | solution.py:309
  8.0 0.0 copy-start.4
  8.0 2.0 fusion.1
  10.0 3.1 %collective-permute-start = (f32[3,16384]{1,0:T(4,128)}, f32[3,16384]{1,0:T(4,128)}, u32[]{:S(2)}, u32[]{:S(2)}) collective-permute-start(f32[3,16384]{1,0:T(4,128)} %get-tuple-element.24), channel_id=1, source_target_pairs={{0,1},{1,2},{2,3},{3,4},{4,5},{5,6},{6,7},{7,8},{8,9},{9,10},{10,1... | collective-permute-start | bytes 589832 | tf_op jit(solution)/shard_map/ppermute | solution.py:309
  13.1 2.7 %collective-permute-start.1 = (f32[3,16384]{1,0:T(4,128)}, f32[3,16384]{1,0:T(4,128)}, u32[]{:S(2)}, u32[]{:S(2)}) collective-permute-start(f32[3,16384]{1,0:T(4,128)} %get-tuple-element.23), channel_id=1, source_target_pairs={{1,0},{2,1},{3,2},{4,3},{5,4},{6,5},{7,6},{8,7},{9,8},{10,9},{11,1... | collective-permute-start | bytes 589832 | tf_op jit(solution)/shard_map/ppermute | solution.py:309
  15.8 0.7 copy.16
  16.5 0.0 copy-done.3
  16.5 0.0 copy-done.2
  16.5 0.0 copy-start
  16.5 2.2 %copy-done = bf16[128,64,256]{2,1,0:T(8,128)(2,1)S(1)} copy-done((bf16[128,64,256]{2,1,0:T(8,128)(2,1)S(1)}, bf16[128,64,256]{2,1,0:T(8,128)(2,1)}, u32[]{:S(2)}) %copy-start) | copy-done | bytes 4194328
  18.7 0.0 copy-start.7
  18.7 0.7 copy-done.7
  19.4 12.0 %moments.1 = (bf16[3072,128]{1,0:T(8,128)(2,1)}, f32[8,64]{1,0:T(8,128)S(1)}) custom-call(s32[6,128]{1,0:T(8,128)S(1)} %bitcast.16, s32[1,128]{1,0:T(1,128)S(1)} %copy-done.7, f32[8,32768]{1,0:T(8,128)S(1)} %copy-done.3, bf16[128,64,256]{2,1,0:T(8,128)(2,1)S(1)} %copy-done, bf16[64,8192]{1,0:T(8,128)(2,1)S(1)} %copy-done.2), custom_call_target="tpu_custom_call" | custom-call | flops 1000000000 | bytes 8388608 | tf_op jit(solution)/shard_map/moments/pallas_call | solution.py:326
  31.4 13.3 %all-to-all-start = ((bf16[128,24,128]{2,1,0:T(8,128)(2,1)}), bf16[128,24,128]{2,1,0:T(8,128)(2,1)S(1)}, u32[]{:S(2)}, u32[]{:S(2)}) async-start(bf16[128,24,128]{2,1,0:T(8,128)(2,1)} %bitcast.4), calls=%async_computation | async-start | bytes 1572864 | tf_op jit(solution)/shard_map/all_to_all | solution.py:338
  44.7 0.0 copy-done.4
  44.7 15.8 %near_self.1.before = f32[8,32768]{1,0:T(8,128)S(1)} custom-call(f32[3,32768]{1,0:T(4,128)S(1)} %copy-done.4, f32[8,32768]{1,0:T(8,128)S(1)} %copy-done.3), custom_call_target="tpu_custom_call" | custom-call | flops 8000000000 | bytes 3145728 | tf_op jit(solution)/shard_map/near_self/pallas_call | solution.py:340
  60.5 0.0 copy-start.8
  60.5 1.0 copy-done.8
  61.5 0.0 copy-start.10
  61.5 22.2 %all_gather.6.gathered = f32[128,64]{1,0:T(8,128)S(1)} all-gather(f32[8,64]{1,0:T(8,128)S(1)} %get-tuple-element.14), channel_id=1, replica_groups=mesh['group'=8,'dev'=16] {'dev'}, dimensions={0}, use_global_device_ids=true | all-gather | bytes 34816 | tf_op jit(solution)/shard_map/all_gather | solution.py:337
  83.8 0.1 pad_add_fusion.place
  83.8 0.0 copy-start.1
  83.8 2.2 %copy-done.1 = f32[254,4096]{1,0:T(8,128)S(1)} copy-done((f32[254,4096]{1,0:T(8,128)S(1)}, f32[254,4096]{1,0:T(8,128)}, u32[]{:S(2)}) %copy-start.1) | copy-done | bytes 4161560
  86.0 0.0 copy-start.6
  86.0 4.2 %group_tree.1 = (f32[4,8,64]{2,1,0:T(8,128)S(1)}, f32[8,64]{1,0:T(8,128)S(1)}) custom-call(s32[2]{0:T(128)S(1)} %pad_add_fusion.place, f32[128,64]{1,0:T(8,128)S(1)} %all_gather.6.gathered, f32[254,4096]{1,0:T(8,128)S(1)} %copy-done.1), custom_call_target="tpu_custom_call" | custom-call | flops 100000000 | bytes 4194304 | tf_op jit(solution)/shard_map/group_tree/pallas_call | solution.py:351
  90.2 0.0 copy-start.5
  90.2 0.6 copy-done.5
  90.8 0.0 copy-done.10
  90.8 0.6 copy.17
  91.4 14.4 %all_gather.7.group_moments = f32[64,64]{1,0:T(8,128)} all-gather(f32[8,64]{1,0:T(8,128)S(1)} %get-tuple-element.19), channel_id=1, replica_groups=mesh['group'=8,'dev'=16] {'group'}, dimensions={0}, use_global_device_ids=true | all-gather | bytes 18432 | tf_op jit(solution)/shard_map/all_gather | solution.py:361
  105.8 0.0 collective-permute-done.2
  105.8 0.8 convert_element_type.10.values_below
  106.7 0.0 collective-permute-done.3
  106.7 0.8 convert_element_type.11.values_above
  107.5 0.0 collective-permute-done.points_below
  107.5 0.0 collective-permute-done.1.points_above
  107.5 77.3 %near_listed.1.near = f32[8,32768]{1,0:T(8,128)} custom-call(s32[6,128]{1,0:T(8,128)} %bitcast.20, f32[3,16384]{1,0:T(4,128)} %collective-permute-done.points_below, f32[3,32768]{1,0:T(4,128)} %points.3, f32[3,16384]{1,0:T(4,128)} %collective-permute-done.1.points_above, f32[8,16384]{1,0:T(8,128)} %convert_element_type.10.values_below, f32[8,32768]{1,0:T(8,128)} %values.5, ...), custom_call_target="tpu_custom_call" | custom-call | flops 60000002048 | bytes 6291456 | tf_op jit(solution)/shard_map/near_listed/pallas_call | solution.py:364
  184.8 0.0 copy-done.6
  184.8 0.0 all-to-all-done
  184.8 0.0 copy-start.9
  184.8 0.9 copy-done.9
  185.7 21.6 %far_field.1 = f32[8,32768]{1,0:T(8,128)} custom-call(s32[2]{0:T(128)} %copy-done.6, s32[6,128]{1,0:T(8,128)} %bitcast.19, bf16[3072,128]{1,0:T(8,128)(2,1)} %bitcast.18, f32[4,8,64]{2,1,0:T(8,128)} %copy-done.5, f32[64,64]{1,0:T(8,128)} %all_gather.7.group_moments, f32[8,32768]{1,0:T(8,128)} %near_listed.1.near, bf16[128,64,384]{2,1,0:T(8,128)(2,1)} %bitcast.17, ...), custom_call_target="tpu_custom_call" | custom-call | flops 2000000000 | bytes 23068672 | tf_op jit(solution)/shard_map/far_field/pallas_call | solution.py:382
Async XLA Ops:
  0.0 16.5 %copy-start.3 = (f32[8,32768]{1,0:T(8,128)S(1)}, f32[8,32768]{1,0:T(8,128)}, u32[]{:S(2)}) copy-start(f32[8,32768]{1,0:T(8,128)} %values.5) | copy-start | bytes 3145732
  0.0 16.5 %copy-start.2 = (bf16[64,8192]{1,0:T(8,128)(2,1)S(1)}, bf16[64,8192]{1,0:T(8,128)(2,1)}, u32[]{:S(2)}) copy-start(bf16[64,8192]{1,0:T(8,128)(2,1)} %transfer_hbm.1) | copy-start | bytes 3145732
  2.2 103.7 %collective-permute-start.2 = (bf16[8,16384]{1,0:T(8,128)(2,1)}, bf16[8,16384]{1,0:T(8,128)(2,1)S(1)}, u32[]{:S(2)}, u32[]{:S(2)}) collective-permute-start(bf16[8,16384]{1,0:T(8,128)(2,1)} %get-tuple-element.22), channel_id=1, source_target_pairs={{0,1},{1,2},{2,3},{3,4},{4,5},{5,6},{6,7},{7,8},{8,9},{9,10},{10,1... | collective-permute-start | bytes 786440 | tf_op jit(solution)/shard_map/ppermute | solution.py:309
  5.3 101.4 %collective-permute-start.3 = (bf16[8,16384]{1,0:T(8,128)(2,1)S(1)}, bf16[8,16384]{1,0:T(8,128)(2,1)S(1)}, u32[]{:S(2)}, u32[]{:S(2)}) collective-permute-start(bf16[8,16384]{1,0:T(8,128)(2,1)S(1)} %get-tuple-element.21), channel_id=1, source_target_pairs={{1,0},{2,1},{3,2},{4,3},{5,4},{6,5},{7,6},{8,7},{9,8},{10,9},{11,1... | collective-permute-start | bytes 786440 | tf_op jit(solution)/shard_map/ppermute | solution.py:309
  8.0 36.7 %copy-start.4 = (f32[3,32768]{1,0:T(4,128)S(1)}, f32[3,32768]{1,0:T(4,128)}, u32[]{:S(2)}) copy-start(f32[3,32768]{1,0:T(4,128)} %points.3) | copy-start | bytes 1179652
  10.0 97.5 %collective-permute-start = (f32[3,16384]{1,0:T(4,128)}, f32[3,16384]{1,0:T(4,128)}, u32[]{:S(2)}, u32[]{:S(2)}) collective-permute-start(f32[3,16384]{1,0:T(4,128)} %get-tuple-element.24), channel_id=1, source_target_pairs={{0,1},{1,2},{2,3},{3,4},{4,5},{5,6},{6,7},{7,8},{8,9},{9,10},{10,1... | collective-permute-start | bytes 589832 | tf_op jit(solution)/shard_map/ppermute | solution.py:309
  13.1 94.4 %collective-permute-start.1 = (f32[3,16384]{1,0:T(4,128)}, f32[3,16384]{1,0:T(4,128)}, u32[]{:S(2)}, u32[]{:S(2)}) collective-permute-start(f32[3,16384]{1,0:T(4,128)} %get-tuple-element.23), channel_id=1, source_target_pairs={{1,0},{2,1},{3,2},{4,3},{5,4},{6,5},{7,6},{8,7},{9,8},{10,9},{11,1... | collective-permute-start | bytes 589832 | tf_op jit(solution)/shard_map/ppermute | solution.py:309
  16.5 2.2 %copy-start = (bf16[128,64,256]{2,1,0:T(8,128)(2,1)S(1)}, bf16[128,64,256]{2,1,0:T(8,128)(2,1)}, u32[]{:S(2)}) copy-start(bf16[128,64,256]{2,1,0:T(8,128)(2,1)} %basis_hbm.1) | copy-start | bytes 12582916
  18.7 0.7 copy-start.7
  31.4 153.4 %all-to-all-start = ((bf16[128,24,128]{2,1,0:T(8,128)(2,1)}), bf16[128,24,128]{2,1,0:T(8,128)(2,1)S(1)}, u32[]{:S(2)}, u32[]{:S(2)}) async-start(bf16[128,24,128]{2,1,0:T(8,128)(2,1)} %bitcast.4), calls=%async_computation | async-start | bytes 1572864 | tf_op jit(solution)/shard_map/all_to_all | solution.py:338
  60.5 1.0 copy-start.8
  61.5 29.3 %copy-start.10 = (s32[1,128,6]{1,0,2:T(1,128)S(1)}, s32[1,128,6]{1,0,2:T(1,128)}, u32[]{:S(2)}) copy-start(s32[1,128,6]{1,0,2:T(1,128)} %param.21) | copy-start | bytes 9220
  83.8 2.2 %copy-start.1 = (f32[254,4096]{1,0:T(8,128)S(1)}, f32[254,4096]{1,0:T(8,128)}, u32[]{:S(2)}) copy-start(f32[254,4096]{1,0:T(8,128)} %top_transfer_hbm.1) | copy-start | bytes 12484612
  86.0 98.8 %copy-start.6 = (s32[2]{0:T(128)}, s32[2]{0:T(128)S(1)}, u32[]{:S(2)}) copy-start(s32[2]{0:T(128)S(1)} %pad_add_fusion.place) | copy-start | bytes 28
  90.2 0.6 copy-start.5
  184.8 0.9 copy-start.9

commit v2 on v1

v2 whole, which is shorter than its diff:
```python
import functools
import math

import jax
import jax.numpy as jnp
from jax import lax
from jax.experimental import pallas as pl
from jax.experimental.pallas import tpu as pltpu
from jax.sharding import PartitionSpec as P

LEAF = 256
R = 64
N = 8
EDGE = 64
OWN = 128
SEEN = 256
SLOTS = 6
NEAR = 6
FEAT = 48
F32 = jnp.float32
BF16 = jnp.bfloat16

kernel_scale = 0.25 / (4.0 * math.pi)
smoothing = 0.0025
inverse_scale = 1.0 / kernel_scale

NN = (((1,), (0,)), ((), ()))
NT = (((1,), (1,)), ((), ()))
VMEM = pl.BlockSpec(memory_space=pltpu.VMEM)
SMEM = pl.BlockSpec(memory_space=pltpu.SMEM)
ANY = pl.BlockSpec(memory_space=pl.ANY)


def dot(a, b, dims=NN):
    return lax.dot_general(a, b, dims, preferred_element_type=F32)


def exact_dot(a, b, dims=NN):
    return lax.dot_general(a, b, dims, precision=lax.Precision.HIGHEST, preferred_element_type=F32)


def aligned(index, size):
    return pl.ds(pl.multiple_of(index * size, size), size)


def params(megabytes):
    return pltpu.CompilerParams(vmem_limit_bytes=megabytes << 20)


def round16(x):
    return x.astype(BF16).astype(F32)


def split_points(points):
    width = points.shape[1]
    row = lax.broadcasted_iota(jnp.int32, (8, width), 0)
    padded = jnp.concatenate([points, jnp.ones((5, width), F32)], 0)
    x = jnp.where(row < 3, (padded - 1.0) * inverse_scale, 0.0)
    high = round16(x)
    return high, round16(x - high)


def features(high, low, is_target):
    width = high.shape[1]
    row = lax.broadcasted_iota(jnp.int32, (8, width), 0)
    x = high + low
    square = jnp.broadcast_to(jnp.sum(x * x, axis=0, keepdims=True), (8, width))
    if is_target:
        square = square + smoothing * inverse_scale * inverse_scale
    s0 = round16(square)
    s1 = round16(square - s0)
    s2 = square - s0 - s1
    zero = jnp.zeros_like(x)
    if is_target:
        last = jnp.where(row == 0, s0, jnp.where(row == 1, s1, jnp.where(row == 2, s2, jnp.where(row < 6, 1.0, 0.0))))
        parts = [-2.0 * high, -2.0 * high, -2.0 * low, -2.0 * low, last, zero]
    else:
        last = jnp.where(row < 3, 1.0, jnp.where(row == 3, s0, jnp.where(row == 4, s1, jnp.where(row == 5, s2, 0.0))))
        parts = [high, low, high, low, last, zero]
    return jnp.concatenate(parts, 0)


def inverse_root(distance):
    return lax.rsqrt(distance.astype(BF16))


def pack_kernel(points, values, first, last):
    rim = EDGE * LEAF
    for out, start in ((first, 0), (last, OWN * LEAF - rim)):

        def one(i, carry):
            columns = pl.ds(pl.multiple_of(start + i * 4 * LEAF, LEAF), 4 * LEAF)
            high, low = split_points(points[:, columns])
            both = high + pltpu.roll(low, 3, 0)
            out[:, aligned(i, 4 * LEAF)] = jnp.concatenate([values[:, columns], both], 0).astype(BF16)
            return carry

        lax.fori_loop(0, EDGE // 4, one, 0)


def moment_kernel(
    place, send_leaf, send_count, values, basis_hbm, transfer, top_transfer_hbm,
    message, basis, top_transfer, moments, chain, matrices, sems,
):
    chunks = 4
    chunk = OWN // chunks
    copies = []
    for i in range(chunks):
        copies.append(pltpu.make_async_copy(basis_hbm.at[pl.ds(i * chunk, chunk)], basis.at[pl.ds(i * chunk, chunk)], sems.at[i]))
    copies.append(pltpu.make_async_copy(top_transfer_hbm, top_transfer, sems.at[chunks]))
    for copy in copies:
        copy.start()
    owner = place[0]

    def four_leaves(g, total):
        picked = []
        for j in range(4):
            leaf = g * 4 + j
            v = values[:, aligned(leaf, LEAF)].astype(BF16)
            m = round16(dot(v, basis[leaf], NT))
            moments[leaf] = jnp.concatenate([m, m], 1)
            picked.append(m)
        return total + dot(jnp.concatenate(picked, 0).astype(BF16), transfer[:, aligned(g, 4 * R)])

    total = jnp.zeros((4 * N, 4 * R), F32)
    for i in range(chunks):
        copies[i].wait()
        total = lax.fori_loop(i * chunk // 4, (i + 1) * chunk // 4, four_leaves, total, unroll=2)
    current = total[0:N, 0:R]
    for j in range(1, 4):
        current = current + total[j * N : (j + 1) * N, j * R : (j + 1) * R]
    current = current * (1.0 / math.sqrt(OWN))

    copies[chunks].wait()
    for level in range(6):
        fetch(top_transfer, 2 * OWN - 2 * (OWN >> level) + (owner >> level), matrices, level)
    for level in range(7):
        high = round16(current)
        chain[level] = jnp.concatenate([high, current - high], 1)
        if level < 6:
            current = exact_dot(current, matrices[level])

    is_left = lax.broadcasted_iota(jnp.int32, (N, 2 * R), 1) < R

    def one_receiver(p, carry):
        rows = []
        count = send_count[0, p]
        for pair in range(SLOTS // 2):
            left = moments[send_leaf[2 * pair, p]]
            right = moments[send_leaf[2 * pair + 1, p]]
            left = jnp.where(2 * pair < count, left, 0.0)
            right = jnp.where(2 * pair + 1 < count, right, 0.0)
            rows.append(jnp.where(is_left, left, right))
        rows.append(chain[top_bit(owner ^ p)])
        message[aligned(p, 4 * N), :] = jnp.concatenate(rows, 0).astype(BF16)
        return carry

    lax.fori_loop(0, OWN, one_receiver, 0, unroll=4)


def top_bit(x):
    return sum((x >= (1 << j)).astype(jnp.int32) for j in range(1, 7))


def near_kernel(
    near_list, below, points, values, above, out, sources, targets, seen_values,
):
    def rim(ref, first):
        row = lax.broadcasted_iota(jnp.int32, (N, LEAF), 0)

        def one(i, carry):
            block = ref[:, aligned(i, LEAF)].astype(F32)
            both = block[N:, :]
            high = jnp.where(row < 3, both, 0.0)
            low = jnp.where(row < 3, pltpu.roll(both, 5, 0), 0.0)
            sources[first + i] = features(high, low, False).T.astype(BF16)
            seen_values[first + i] = block[:N, :]
            return carry

        lax.fori_loop(0, EDGE, one, 0, unroll=2)

    def own(i, carry):
        high, low = split_points(points[:, aligned(i, LEAF)])
        sources[EDGE + i] = features(high, low, False).T.astype(BF16)
        targets[i] = features(high, low, True).astype(BF16)
        seen_values[EDGE + i] = values[:, aligned(i, LEAF)]
        return carry

    lax.fori_loop(0, OWN, own, 0, unroll=2)
    rim(below, 0)
    rim(above, EDGE + OWN)

    def two_leaves(g, carry):
        for j in range(2):
            leaf = g * 2 + j
            target = targets[leaf]
            seen = [EDGE + leaf] + [near_list[k, leaf] for k in range(NEAR)]
            kernels = [inverse_root(dot(sources[e], target)) for e in seen]
            total = jnp.zeros((N, LEAF), F32)
            for e, kernel in zip(seen, kernels):
                total = total + dot(seen_values[e].astype(BF16), kernel)
            out[:, aligned(leaf, LEAF)] = total
        return carry

    lax.fori_loop(0, OWN // 2, two_leaves, 0)


def fetch(table, row, matrices, slot):
    flat = table[pl.ds(row, 1), :]
    for j in range(R // 2):
        pair = flat[:, j * 2 * R : (j + 1) * 2 * R]
        matrices[slot, 2 * j : 2 * j + 1, 0:R] = pair[:, 0:R]
        matrices[slot, 2 * j + 1 : 2 * j + 2, 0:R] = pair[:, R : 2 * R]


def far_kernel(
    place, far_target, incoming, near,
    coupling_hbm, transfer_hbm, basis_hbm, top_transfer_hbm, top_coupling_hbm,
    out,
    coupling, transfer, basis, top_transfer, top_coupling, far_local, matrices, siblings, sems,
):
    chunks = 4
    chunk = OWN // chunks
    copies = []
    for i in range(chunks):
        copies.append(pltpu.make_async_copy(coupling_hbm.at[pl.ds(i * chunk, chunk)], coupling.at[pl.ds(i * chunk, chunk)], sems.at[i]))
    rest = [(top_transfer_hbm, top_transfer), (top_coupling_hbm, top_coupling), (transfer_hbm, transfer), (basis_hbm, basis)]
    for i, (source, target) in enumerate(rest):
        copies.append(pltpu.make_async_copy(source, target, sems.at[chunks + i]))
    for copy in copies:
        copy.start()

    owner = place[0]
    far_local[...] = jnp.zeros_like(far_local)
    siblings[...] = jnp.zeros_like(siblings)
    is_left = lax.broadcasted_iota(jnp.int32, (N, 2 * R), 1) < R

    for i in range(chunks):
        copies[i].wait()

        def two_senders(g, carry):
            arrived = incoming[aligned(g, 64), :].astype(F32)
            results = []
            for j in range(2):
                p = g * 2 + j
                for pair in range(SLOTS // 2):
                    tile = arrived[(j * 4 + pair) * N : (j * 4 + pair + 1) * N, :]
                    left = jnp.where(is_left, tile, 0.0)
                    right = jnp.where(is_left, 0.0, tile)
                    both = jnp.concatenate([left, right], 0).astype(BF16)
                    matrix = coupling[p, :, pair * 2 * R : (pair + 1) * 2 * R]
                    results.append(dot(both, matrix, NT))
            for j in range(2):
                p = g * 2 + j
                level = jnp.where(p == owner, 7, top_bit(owner ^ p))
                siblings[level] = siblings[level] + arrived[(j * 4 + 3) * N : (j * 4 + 4) * N, :]
                for slot in range(SLOTS):
                    leaf = far_target[slot, p]
                    part = results[j * 3 + slot // 2][(slot % 2) * N : (slot % 2 + 1) * N, :]
                    far_local[leaf] = far_local[leaf] + part
            return carry

        lax.fori_loop(i * chunk // 2, (i + 1) * chunk // 2, two_senders, 0, unroll=2)

    copies[chunks].wait()
    copies[chunks + 1].wait()
    for level in range(7):
        node = 2 * OWN - 2 * (OWN >> level) + (owner >> level)
        fetch(top_coupling, node, matrices, level)
        if level < 6:
            fetch(top_transfer, node, matrices, 7 + level)
    coupled = []
    for level in range(7):
        both = siblings[level]
        coupled.append(exact_dot(both[:, :R] + both[:, R:], matrices[level], NT))
    field = coupled[6]
    for level in reversed(range(6)):
        field = coupled[level] + exact_dot(field, matrices[7 + level], NT)
    field = round16(field)

    wide = jnp.concatenate([jnp.concatenate([field] * 4, 1)] * 4, 0)
    row_leaf = lax.broadcasted_iota(jnp.int32, (4 * N, 4 * R), 0) // N
    column_leaf = lax.broadcasted_iota(jnp.int32, (4 * N, 4 * R), 1) // R
    fields = jnp.where(row_leaf == column_leaf, wide, 0.0).astype(BF16)
    copies[chunks + 2].wait()
    copies[chunks + 3].wait()

    def four_leaves(g, carry):
        local = dot(fields, transfer[:, aligned(g, 4 * R)], NT)
        for j in range(4):
            leaf = g * 4 + j
            total = (local[j * N : (j + 1) * N, :] + far_local[leaf]).astype(BF16)
            out[:, aligned(leaf, LEAF)] = near[:, aligned(leaf, LEAF)] + dot(total, basis[leaf])
        return carry

    lax.fori_loop(0, OWN // 4, four_leaves, 0, unroll=2)


def from_behind(block, axis, distance):
    devices = range(lax.axis_size(axis))
    route = [(i - distance, i) for i in devices if i - distance in devices]
    return lax.ppermute(block, axis, route)


def shards(
    positions, right_sides, leaf_basis, leaf_transfer, far_coupling, top_transfer, top_coupling,
    near_list, send_leaf, send_count, far_target,
):
    both = ("group", "dev")
    points = OWN * LEAF
    rim = EDGE * LEAF
    place = (lax.axis_index("group") * lax.axis_size("dev") + lax.axis_index("dev")).astype(jnp.int32).reshape(1)

    first, last = pl.pallas_call(
        pack_kernel,
        out_shape=(jax.ShapeDtypeStruct((2 * N, rim), BF16),) * 2,
        in_specs=[VMEM, VMEM],
        out_specs=(VMEM, VMEM),
        compiler_params=params(16),
        cost_estimate=pl.CostEstimate(flops=10**7, bytes_accessed=3 << 20, transcendentals=0),
        name="pack",
    )(positions, right_sides)
    below = from_behind(last, both, 1)
    above = from_behind(first, both, -1)

    message = pl.pallas_call(
        moment_kernel,
        out_shape=jax.ShapeDtypeStruct((OWN * 4 * N, 2 * R), BF16),
        in_specs=[SMEM, SMEM, SMEM, VMEM, ANY, VMEM, ANY],
        out_specs=VMEM,
        scratch_shapes=[
            pltpu.VMEM((OWN, R, LEAF), BF16),
            pltpu.VMEM((254, R * R), F32),
            pltpu.VMEM((OWN, N, 2 * R), F32),
            pltpu.VMEM((7, N, 2 * R), F32),
            pltpu.VMEM((6, R, R), F32),
            pltpu.SemaphoreType.DMA((5,)),
        ],
        compiler_params=params(32),
        cost_estimate=pl.CostEstimate(flops=10**9, bytes_accessed=12 << 20, transcendentals=0),
        name="moments",
    )(place, send_leaf[0].T, send_count, right_sides, leaf_basis, leaf_transfer, top_transfer)
    incoming = lax.all_to_all(message, both, split_axis=0, concat_axis=0, tiled=True)

    near = pl.pallas_call(
        near_kernel,
        out_shape=jax.ShapeDtypeStruct((N, points), F32),
        in_specs=[SMEM] + [VMEM] * 4,
        out_specs=VMEM,
        scratch_shapes=[
            pltpu.VMEM((SEEN, LEAF, FEAT), BF16),
            pltpu.VMEM((OWN, FEAT, LEAF), BF16),
            pltpu.VMEM((SEEN, N, LEAF), F32),
        ],
        compiler_params=params(56),
        cost_estimate=pl.CostEstimate(flops=60 * 10**9, bytes_accessed=6 << 20, transcendentals=0),
        name="near",
    )(near_list.T, below, positions, right_sides, above)

    return pl.pallas_call(
        far_kernel,
        out_shape=jax.ShapeDtypeStruct((N, points), F32),
        in_specs=[SMEM, SMEM, VMEM, VMEM, ANY, ANY, ANY, ANY, ANY],
        out_specs=VMEM,
        scratch_shapes=[
            pltpu.VMEM((OWN, R, SLOTS * R), BF16),
            pltpu.VMEM((R, OWN * R), BF16),
            pltpu.VMEM((OWN, R, LEAF), BF16),
            pltpu.VMEM((254, R * R), F32),
            pltpu.VMEM((254, R * R), F32),
            pltpu.VMEM((OWN, N, R), F32),
            pltpu.VMEM((13, R, R), F32),
            pltpu.VMEM((8, N, 2 * R), F32),
            pltpu.SemaphoreType.DMA((8,)),
        ],
        compiler_params=params(56),
        cost_estimate=pl.CostEstimate(flops=2 * 10**9, bytes_accessed=22 << 20, transcendentals=0),
        name="far_field",
    )(place, far_target[0].T, incoming, near, far_coupling[0], leaf_transfer, leaf_basis, top_transfer, top_coupling)


def solution(mesh):
    both = ("group", "dev")
    placed = (
        P(None, both), P(None, both), P(both, None, None), P(None, both), P(both, None, None, None),
        P(), P(), P(both, None), P(both, None, None), P(both, None), P(both, None, None),
    )
    return jax.shard_map(shards, mesh=mesh, in_specs=placed, out_specs=P(None, both), check_vma=False)
```

time: 211 us -> 143 us (0.68); the launches traced: 207 us -> 141 us
  blocking collectives: 36.7 us -> 0 us
  Pallas kernels: 131 us -> 112 us
  starting transfers between devices: 24.9 us -> 16.3 us
  other arithmetic: 3.17 us -> 0 us
    all_gather x2 -> x0, blocking collectives: 36.7 us -> none  [the longest x1 22.2 us: shards(): gathered = lax.all_gather(device_moment, 'dev', axis=0, tiled=True)]
    pallas_call x3 -> x2, Pallas kernels: 32 us -> 13.3 us  [the longest x1 12.7 us: shards(): pl.pallas_call(moment_kernel, out_shape=jax.ShapeDtypeStruct((OWN * 4 * N...]
    ppermute x4 -> x2, starting transfers between devices: 11.7 us -> 5.84 us  [from_behind(): return lax.ppermute(block, axis, route)]
    unnamed x24, local copies, waits for them, and re-layouts: 8.81 us -> 13 us
    convert_element_type x3 -> x0, other arithmetic: 3.1 us -> none  [the longest x1 1.43 us: shards(): rounded = right_sides.astype(BF16)]
    all_to_all x1, starting transfers between devices: 13.3 us -> 10.5 us  [shards(): lax.all_to_all(message, both, split_axis=0, concat_axis=0, tiled=True)]
    slice x2 -> x0, local copies, waits for them, and re-layouts: 2.71 us -> none  [the longest x1 1.97 us: shards(): points_above = from_behind(positions[:, :rim], both, -1)]
  transfers between devices with their start and end apart: 5 -> 3, of which waited for: 0 -> 0; matrix products, arithmetic and copies ran while one was open for 2% -> 1% of each run, Pallas kernels for 53% -> 64%
where the time goes in v2:
time: 143 us; the launch traced here: 141 us
  Pallas kernels  112 us (78%)
  starting transfers between devices  16.3 us (11%)
  local copies, waits for them, and re-layouts  13 us (9%)
    pallas_call x1, Pallas kernels, shards(): pl.pallas_call(near_kernel, out_shape=jax.ShapeDtypeStruct((N, points), F...  78.5 us
    pallas_call x1, Pallas kernels, shards(): pl.pallas_call(far_kernel, out_shape=jax.ShapeDtypeStruct((N, points), F3...  20.2 us
    unnamed x24, local copies, waits for them, and re-layouts  13 us
    pallas_call x1, Pallas kernels, shards(): pl.pallas_call(moment_kernel, out_shape=jax.ShapeDtypeStruct((OWN * 4 * N...  12.7 us
    all_to_all x1, starting transfers between devices, shards(): lax.all_to_all(message, both, split_axis=0, concat_axis=0, tiled=True)  10.5 us
    ppermute x2, starting transfers between devices, from_behind(): return lax.ppermute(block, axis, route)  5.84 us
  transfers between devices with their start and end apart: 3, of which 0 were waited for; matrix products, arithmetic and copies ran while one was open for 1% of the time, Pallas kernels for 64%

profile of v2, /device:TPU:4, one launch (start us, length us, event | category | flops | bytes accessed | tf_op | source)
XLA Modules:
  0.0 141.5 jit_solution(9531773483647924644)
XLA Ops:
  0.0 0.0 copy-start.3
  0.0 1.2 copy-done.3
  1.2 0.0 copy-start.5
  1.2 1.0 copy-done.5
  2.3 0.7 pack.1
  3.0 3.1 %collective-permute-start = (bf16[16,16384]{1,0:T(8,128)(2,1)S(1)}, bf16[16,16384]{1,0:T(8,128)(2,1)S(1)}, u32[]{:S(2)}, u32[]{:S(2)}) collective-permute-start(bf16[16,16384]{1,0:T(8,128)(2,1)S(1)} %get-tuple-element.7), channel_id=1, source_target_pairs={{0,1},{1,2},{2,3},{3,4},{4,5},{5,6},{6,7},{7,8},{8,9},{9,10},{10,1... | collective-permute-start | bytes 1572872 | tf_op jit(solution)/shard_map/ppermute | solution.py:302
  6.1 2.7 %collective-permute-start.1 = (bf16[16,16384]{1,0:T(8,128)(2,1)S(1)}, bf16[16,16384]{1,0:T(8,128)(2,1)S(1)}, u32[]{:S(2)}, u32[]{:S(2)}) collective-permute-start(bf16[16,16384]{1,0:T(8,128)(2,1)S(1)} %get-tuple-element.8), channel_id=1, source_target_pairs={{1,0},{2,1},{3,2},{4,3},{5,4},{6,5},{7,6},{8,7},{9,8},{10,9},{11,1... | collective-permute-start | bytes 1572872 | tf_op jit(solution)/shard_map/ppermute | solution.py:302
  8.8 0.7 copy.16
  9.5 0.0 copy-start
  9.5 2.2 %copy-done = bf16[128,64,256]{2,1,0:T(8,128)(2,1)S(1)} copy-done((bf16[128,64,256]{2,1,0:T(8,128)(2,1)S(1)}, bf16[128,64,256]{2,1,0:T(8,128)(2,1)}, u32[]{:S(2)}) %copy-start) | copy-done | bytes 4194328
  11.7 0.0 copy-start.1
  11.7 2.2 %copy-done.1 = f32[254,4096]{1,0:T(8,128)S(1)} copy-done((f32[254,4096]{1,0:T(8,128)S(1)}, f32[254,4096]{1,0:T(8,128)}, u32[]{:S(2)}) %copy-start.1) | copy-done | bytes 4161560
  13.9 0.0 copy-start.2
  13.9 1.2 copy-done.2
  15.1 0.0 copy-start.4
  15.1 1.2 copy-done.4
  16.3 0.0 copy-start.6
  16.3 0.7 copy-done.6
  17.0 0.0 copy-start.8
  17.0 12.7 %moments.1 = bf16[4096,128]{1,0:T(8,128)(2,1)} custom-call(s32[1]{0:T(128)} %bitcast.place, s32[6,128]{1,0:T(8,128)S(1)} %bitcast.15, s32[1,128]{1,0:T(1,128)S(1)} %copy-done.6, f32[8,32768]{1,0:T(8,128)S(1)} %copy-done.4, bf16[128,64,256]{2,1,0:T(8,128)(2,1)S(1)} %copy-done, bf16[64,8192]{1,0:T(8,128)(2,1)S(1)} %copy-done.2, f32[254,4096]{1,0:T(8,128)S(1)} %copy-done.1), custom_call_target="tpu_custom_call" | custom-call | flops 1000000000 | bytes 12582912 | tf_op jit(solution)/shard_map/moments/pallas_call | solution.py:326
  29.7 10.5 %all-to-all-start = ((bf16[128,32,128]{2,1,0:T(8,128)(2,1)}), bf16[128,32,128]{2,1,0:T(8,128)(2,1)S(1)}, u32[]{:S(2)}, u32[]{:S(2)}) async-start(bf16[128,32,128]{2,1,0:T(8,128)(2,1)} %bitcast.3), calls=%async_computation | async-start | bytes 2097152 | tf_op jit(solution)/shard_map/all_to_all | solution.py:343
  40.2 0.0 copy-done.8
  40.2 0.6 copy.17
  40.8 0.0 collective-permute-done.below
  40.8 0.0 copy-start.9
  40.8 0.0 collective-permute-done.1.above
  40.8 0.0 copy-start.10
  40.8 0.8 copy-done.9
  41.6 0.2 copy-done.10
  41.8 78.5 %near.1 = f32[8,32768]{1,0:T(8,128)} custom-call(s32[6,128]{1,0:T(8,128)} %bitcast.19, bf16[16,16384]{1,0:T(8,128)(2,1)} %copy-done.9, f32[3,32768]{1,0:T(4,128)} %points.3, f32[8,32768]{1,0:T(8,128)} %values.5, bf16[16,16384]{1,0:T(8,128)(2,1)} %copy-done.10), custom_call_target="tpu_custom_call" | custom-call | flops 60000002048 | bytes 6291456 | tf_op jit(solution)/shard_map/near/pallas_call | solution.py:345
  120.2 0.0 all-to-all-done
  120.2 0.0 copy-start.7
  120.2 1.0 copy-done.7
  121.2 20.2 %far_field.1 = f32[8,32768]{1,0:T(8,128)} custom-call(s32[1]{0:T(128)} %bitcast.place, s32[6,128]{1,0:T(8,128)} %bitcast.18, bf16[4096,128]{1,0:T(8,128)(2,1)} %bitcast.17, f32[8,32768]{1,0:T(8,128)} %near.1, bf16[128,64,384]{2,1,0:T(8,128)(2,1)} %bitcast.16, bf16[64,8192]{1,0:T(8,128)(2,1)} %transfer_hbm.1, bf16[128,64,256]{2,1,0:T(8,128)(2,1)} %basis_hbm.3, ...), custom_call_target="tpu_custom_call" | custom-call | flops 2000000000 | bytes 23068672 | tf_op jit(solution)/shard_map/far_field/pallas_call | solution.py:360
Async XLA Ops:
  0.0 1.2 copy-start.3
  1.2 1.0 copy-start.5
  3.0 37.8 %collective-permute-start = (bf16[16,16384]{1,0:T(8,128)(2,1)S(1)}, bf16[16,16384]{1,0:T(8,128)(2,1)S(1)}, u32[]{:S(2)}, u32[]{:S(2)}) collective-permute-start(bf16[16,16384]{1,0:T(8,128)(2,1)S(1)} %get-tuple-element.7), channel_id=1, source_target_pairs={{0,1},{1,2},{2,3},{3,4},{4,5},{5,6},{6,7},{7,8},{8,9},{9,10},{10,1... | collective-permute-start | bytes 1572872 | tf_op jit(solution)/shard_map/ppermute | solution.py:302
  6.1 34.7 %collective-permute-start.1 = (bf16[16,16384]{1,0:T(8,128)(2,1)S(1)}, bf16[16,16384]{1,0:T(8,128)(2,1)S(1)}, u32[]{:S(2)}, u32[]{:S(2)}) collective-permute-start(bf16[16,16384]{1,0:T(8,128)(2,1)S(1)} %get-tuple-element.8), channel_id=1, source_target_pairs={{1,0},{2,1},{3,2},{4,3},{5,4},{6,5},{7,6},{8,7},{9,8},{10,9},{11,1... | collective-permute-start | bytes 1572872 | tf_op jit(solution)/shard_map/ppermute | solution.py:302
  9.5 2.2 %copy-start = (bf16[128,64,256]{2,1,0:T(8,128)(2,1)S(1)}, bf16[128,64,256]{2,1,0:T(8,128)(2,1)}, u32[]{:S(2)}) copy-start(bf16[128,64,256]{2,1,0:T(8,128)(2,1)} %basis_hbm.3) | copy-start | bytes 12582916
  11.7 2.2 %copy-start.1 = (f32[254,4096]{1,0:T(8,128)S(1)}, f32[254,4096]{1,0:T(8,128)}, u32[]{:S(2)}) copy-start(f32[254,4096]{1,0:T(8,128)} %top_transfer_hbm.3) | copy-start | bytes 12484612
  13.9 1.2 copy-start.2
  15.1 1.2 copy-start.4
  16.3 0.7 copy-start.6
  17.0 23.2 %copy-start.8 = (s32[1,128,6]{1,0,2:T(1,128)S(1)}, s32[1,128,6]{1,0,2:T(1,128)}, u32[]{:S(2)}) copy-start(s32[1,128,6]{1,0,2:T(1,128)} %param.21) | copy-start | bytes 9220
  29.7 90.6 %all-to-all-start = ((bf16[128,32,128]{2,1,0:T(8,128)(2,1)}), bf16[128,32,128]{2,1,0:T(8,128)(2,1)S(1)}, u32[]{:S(2)}, u32[]{:S(2)}) async-start(bf16[128,32,128]{2,1,0:T(8,128)(2,1)} %bitcast.3), calls=%async_computation | async-start | bytes 2097152 | tf_op jit(solution)/shard_map/all_to_all | solution.py:343
  40.8 0.8 copy-start.9
  40.8 1.0 copy-start.10
  120.2 1.0 copy-start.7

commit v3 on v2

v3 whole, which is shorter than its diff:
```python
import functools
import math

import jax
import jax.numpy as jnp
from jax import lax
from jax.experimental import pallas as pl
from jax.experimental.pallas import tpu as pltpu
from jax.sharding import PartitionSpec as P

LEAF = 256
R = 64
N = 8
EDGE = 64
OWN = 128
SEEN = 256
SLOTS = 6
NEAR = 6
FEAT = 32
F32 = jnp.float32
BF16 = jnp.bfloat16

kernel_scale = 0.25 / (4.0 * math.pi)
smoothing = 0.0025
inverse_scale = 1.0 / kernel_scale

NN = (((1,), (0,)), ((), ()))
NT = (((1,), (1,)), ((), ()))
VMEM = pl.BlockSpec(memory_space=pltpu.VMEM)
SMEM = pl.BlockSpec(memory_space=pltpu.SMEM)
ANY = pl.BlockSpec(memory_space=pl.ANY)


def dot(a, b, dims=NN):
    return lax.dot_general(a, b, dims, preferred_element_type=F32)


def exact_dot(a, b, dims=NN):
    return lax.dot_general(a, b, dims, precision=lax.Precision.HIGHEST, preferred_element_type=F32)


def aligned(index, size):
    return pl.ds(pl.multiple_of(index * size, size), size)


def params(megabytes):
    return pltpu.CompilerParams(vmem_limit_bytes=megabytes << 20)


def round16(x):
    return x.astype(BF16).astype(F32)


def split_points(points):
    width = points.shape[1]
    row = lax.broadcasted_iota(jnp.int32, (N, width), 0)
    padded = jnp.concatenate([points, jnp.ones((5, width), F32)], 0)
    x = jnp.where(row < 3, (padded - 1.0) * inverse_scale, 0.0)
    high = round16(x)
    return high + pltpu.roll(round16(x - high), 3, 0)


def square_parts(parts, swapped, offset):
    row = lax.broadcasted_iota(jnp.int32, parts.shape, 0)
    x = jnp.where(row < 3, parts + swapped, 0.0)
    square = jnp.broadcast_to(jnp.sum(x * x, axis=0, keepdims=True), parts.shape) + offset
    s0 = round16(square)
    s1 = round16(square - s0)
    return row, s0, s1, square - s0 - s1


def swap_parts(parts):
    row = lax.broadcasted_iota(jnp.int32, parts.shape, 0)
    return jnp.where(row < 3, pltpu.roll(parts, 5, 0), pltpu.roll(parts, 3, 0))


def source_features(parts):
    row, s0, s1, s2 = square_parts(parts, swap_parts(parts), 0.0)
    first = jnp.where(row < 6, parts, 1.0)
    second = jnp.where(row < 6, parts, jnp.where(row == 6, s0, s1))
    third = jnp.where(row == 0, 1.0, jnp.where(row == 1, s2, 0.0))
    return jnp.concatenate([first, second, third, jnp.zeros_like(parts)], 0).astype(BF16).T


def target_features(parts):
    swapped = swap_parts(parts)
    row, s0, s1, s2 = square_parts(parts, swapped, smoothing * inverse_scale * inverse_scale)
    first = jnp.where(row < 6, -2.0 * parts, jnp.where(row == 6, s0, s1))
    second = jnp.where(row < 6, -2.0 * swapped, 1.0)
    third = jnp.where(row == 0, s2, jnp.where(row == 1, 1.0, 0.0))
    return jnp.concatenate([first, second, third, jnp.zeros_like(parts)], 0).astype(BF16)


def inverse_root(distance):
    return lax.rsqrt(distance).astype(BF16)


def pack_kernel(points_hbm, values_hbm, first, last, points, values, sems):
    chunks = 4
    width = OWN * LEAF // chunks
    copies = []
    for i in range(chunks):
        some = pl.ds(i * width, width)
        copies.append(pltpu.make_async_copy(points_hbm.at[:, some], points.at[:, some], sems.at[2 * i]))
        copies.append(pltpu.make_async_copy(values_hbm.at[:, some], values.at[:, some], sems.at[2 * i + 1]))
    for copy in copies:
        copy.start()
    for i in range(chunks):
        copies[2 * i].wait()
        copies[2 * i + 1].wait()
        for j in range(i * width, (i + 1) * width, 4 * LEAF):
            some = slice(j, j + 4 * LEAF)
            out, start = (first, j) if j < EDGE * LEAF else (last, j - EDGE * LEAF)
            rows = jnp.concatenate([values[:, some], split_points(points[:, some])], 0)
            out[:, start : start + 4 * LEAF] = rows.astype(BF16)


def top_bit(x):
    return jnp.maximum(31 - lax.clz(x), 0)


def node_of(owner, level):
    return 2 * OWN - 2 * (OWN >> level) + lax.shift_right_logical(owner, level)


def path_copies(table, rows, owner, sems, first):
    copies = []
    for level in range(5):
        start = pl.multiple_of(lax.shift_right_logical(node_of(owner, level), 3) * 8, 8)
        copies.append(pltpu.make_async_copy(table.at[pl.ds(start, 8)], rows.at[level], sems.at[first + level]))
    copies.append(pltpu.make_async_copy(table.at[pl.ds(248, 6)], rows.at[5, pl.ds(0, 6)], sems.at[first + 5]))
    return copies


def path_matrix(rows, owner, level, matrices, slot):
    node = node_of(owner, level)
    fetch(rows.at[min(level, 5)], lax.bitwise_and(node, 7), matrices, slot)


def moment_kernel(
    place, send_leaf, send_count, values_hbm, basis_hbm, transfer_hbm, top_transfer_hbm,
    message, values, basis, transfer, rows, moments, chain, matrices, sems,
):
    owner = place[0]
    chunks = 4
    chunk = OWN // chunks
    copies = []
    for i in range(chunks):
        some = pl.ds(i * chunk * LEAF, chunk * LEAF)
        copies.append(pltpu.make_async_copy(values_hbm.at[:, some], values.at[:, some], sems.at[3 * i]))
        some = pl.ds(i * chunk, chunk)
        copies.append(pltpu.make_async_copy(basis_hbm.at[some], basis.at[some], sems.at[3 * i + 1]))
        some = pl.ds(i * chunk * R, chunk * R)
        copies.append(pltpu.make_async_copy(transfer_hbm.at[:, some], transfer.at[:, some], sems.at[3 * i + 2]))
    paths = path_copies(top_transfer_hbm, rows, owner, sems, 3 * chunks)
    for copy in copies + paths:
        copy.start()

    def some_leaves(g, total):
        picked = []
        for j in range(16):
            leaf = g * 16 + j
            v = values[:, aligned(leaf, LEAF)].astype(BF16)
            picked.append(round16(dot(v, basis[leaf], NT)))
        for j in range(16):
            moments[g * 16 + j] = jnp.concatenate([picked[j], picked[j]], 1)
        for j in range(0, 16, 4):
            four = jnp.concatenate(picked[j : j + 4], 0).astype(BF16)
            total = total + dot(four, transfer[:, aligned(g * 4 + j // 4, 4 * R)])
        return total

    total = jnp.zeros((4 * N, 4 * R), F32)
    for i in range(chunks):
        for copy in copies[3 * i : 3 * i + 3]:
            copy.wait()
        total = lax.fori_loop(i * chunk // 16, (i + 1) * chunk // 16, some_leaves, total)
    current = total[0:N, 0:R]
    for j in range(1, 4):
        current = current + total[j * N : (j + 1) * N, j * R : (j + 1) * R]
    current = current * (1.0 / math.sqrt(OWN))

    for copy in paths:
        copy.wait()
    for level in range(6):
        path_matrix(rows, owner, level, matrices, level)
    for level in range(7):
        high = round16(current)
        chain[level] = jnp.concatenate([high, current - high], 1)
        if level < 6:
            current = exact_dot(current, matrices[level])

    is_left = lax.broadcasted_iota(jnp.int32, (N, 2 * R), 1) < R

    def one_receiver(p, carry):
        parts = []
        count = send_count[0, p]
        for pair in range(SLOTS // 2):
            left = moments[send_leaf[2 * pair, p]]
            right = moments[send_leaf[2 * pair + 1, p]]
            left = jnp.where(2 * pair < count, left, 0.0)
            right = jnp.where(2 * pair + 1 < count, right, 0.0)
            parts.append(jnp.where(is_left, left, right))
        parts.append(chain[top_bit(owner ^ p)])
        message[aligned(p, 4 * N), :] = jnp.concatenate(parts, 0).astype(BF16)
        return carry

    lax.fori_loop(0, OWN, one_receiver, 0, unroll=8)


def near_kernel(
    near_list, below, points, values, above, out, sources, targets, seen_values,
):
    def rim(ref, first):
        def one(i, carry):
            block = ref[:, aligned(i, LEAF)].astype(F32)
            sources[first + i] = source_features(block[N:, :])
            seen_values[first + i] = block[:N, :]
            return carry

        lax.fori_loop(0, EDGE, one, 0, unroll=4)

    def own(i, carry):
        parts = split_points(points[:, aligned(i, LEAF)])
        sources[EDGE + i] = source_features(parts)
        targets[i] = target_features(parts)
        seen_values[EDGE + i] = values[:, aligned(i, LEAF)]
        return carry

    lax.fori_loop(0, OWN, own, 0, unroll=4)
    rim(below, 0)
    rim(above, EDGE + OWN)

    def finish(leaf, seen, kernels):
        total = dot(seen_values[seen[0]].astype(BF16), kernels[0])
        for e, kernel in zip(seen[1:], kernels[1:]):
            total = total + dot(seen_values[e].astype(BF16), kernel)
        out[:, aligned(leaf, LEAF)] = total

    def eight_leaves(g, carry):
        waiting = None
        for j in range(8):
            leaf = g * 8 + j
            target = targets[leaf]
            seen = [EDGE + leaf] + [near_list[k, leaf] for k in range(NEAR)]
            kernels = [inverse_root(dot(sources[e], target)) for e in seen]
            if waiting is not None:
                finish(*waiting)
            waiting = (leaf, seen, kernels)
        finish(*waiting)
        return carry

    lax.fori_loop(0, OWN // 8, eight_leaves, 0)


def fetch(table, row, matrices, slot):
    flat = table[pl.ds(row, 1), :]
    for j in range(R // 2):
        pair = flat[:, j * 2 * R : (j + 1) * 2 * R]
        matrices[slot, 2 * j : 2 * j + 1, 0:R] = pair[:, 0:R]
        matrices[slot, 2 * j + 1 : 2 * j + 2, 0:R] = pair[:, R : 2 * R]


def far_kernel(
    place, far_target, incoming, near,
    coupling_hbm, transfer_hbm, basis_hbm, top_transfer_hbm, top_coupling_hbm,
    out,
    coupling, transfer, basis, transfer_rows, coupling_rows, far_local, matrices, siblings, sems,
):
    owner = place[0]
    chunks = 4
    chunk = OWN // chunks
    copies = []
    for i in range(chunks):
        copies.append(pltpu.make_async_copy(coupling_hbm.at[pl.ds(i * chunk, chunk)], coupling.at[pl.ds(i * chunk, chunk)], sems.at[i]))
    copies.append(pltpu.make_async_copy(transfer_hbm, transfer, sems.at[chunks]))
    copies.append(pltpu.make_async_copy(basis_hbm, basis, sems.at[chunks + 1]))
    paths = path_copies(top_transfer_hbm, transfer_rows, owner, sems, chunks + 2)
    paths = paths + path_copies(top_coupling_hbm, coupling_rows, owner, sems, chunks + 8)
    for copy in copies[:chunks] + paths + copies[chunks:]:
        copy.start()

    far_local[...] = jnp.zeros_like(far_local)
    siblings[...] = jnp.zeros_like(siblings)
    is_left = lax.broadcasted_iota(jnp.int32, (N, 2 * R), 1) < R

    for i in range(chunks):
        copies[i].wait()

        def two_senders(g, carry):
            arrived = incoming[aligned(g, 64), :].astype(F32)
            results = []
            for j in range(2):
                p = g * 2 + j
                for pair in range(SLOTS // 2):
                    tile = arrived[(j * 4 + pair) * N : (j * 4 + pair + 1) * N, :]
                    left = jnp.where(is_left, tile, 0.0)
                    right = jnp.where(is_left, 0.0, tile)
                    both = jnp.concatenate([left, right], 0).astype(BF16)
                    matrix = coupling[p, :, pair * 2 * R : (pair + 1) * 2 * R]
                    results.append(dot(both, matrix, NT))
            for j in range(2):
                p = g * 2 + j
                level = jnp.where(p == owner, 7, top_bit(owner ^ p))
                siblings[level] = siblings[level] + arrived[(j * 4 + 3) * N : (j * 4 + 4) * N, :]
                for slot in range(SLOTS):
                    leaf = far_target[slot, p]
                    part = results[j * 3 + slot // 2][(slot % 2) * N : (slot % 2 + 1) * N, :]
                    far_local[leaf] = far_local[leaf] + part
            return carry

        lax.fori_loop(i * chunk // 2, (i + 1) * chunk // 2, two_senders, 0, unroll=4)

    for copy in paths:
        copy.wait()
    for level in range(7):
        path_matrix(coupling_rows, owner, level, matrices, level)
        if level < 6:
            path_matrix(transfer_rows, owner, level, matrices, 7 + level)
    coupled = []
    for level in range(7):
        both = siblings[level]
        coupled.append(exact_dot(both[:, :R] + both[:, R:], matrices[level], NT))
    field = coupled[6]
    for level in reversed(range(6)):
        field = coupled[level] + exact_dot(field, matrices[7 + level], NT)
    field = round16(field)

    wide = jnp.concatenate([jnp.concatenate([field] * 4, 1)] * 4, 0)
    row_leaf = lax.broadcasted_iota(jnp.int32, (4 * N, 4 * R), 0) // N
    column_leaf = lax.broadcasted_iota(jnp.int32, (4 * N, 4 * R), 1) // R
    fields = jnp.where(row_leaf == column_leaf, wide, 0.0).astype(BF16)
    copies[chunks].wait()
    copies[chunks + 1].wait()

    def some_leaves(g, carry):
        locals_ = []
        for i in range(4):
            locals_.append(dot(fields, transfer[:, aligned(g * 4 + i, 4 * R)], NT))
        for j in range(16):
            leaf = g * 16 + j
            total = (locals_[j // 4][(j % 4) * N : (j % 4 + 1) * N, :] + far_local[leaf]).astype(BF16)
            out[:, aligned(leaf, LEAF)] = near[:, aligned(leaf, LEAF)] + dot(total, basis[leaf])
        return carry

    lax.fori_loop(0, OWN // 16, some_leaves, 0)


def from_behind(block, axis, distance):
    devices = range(lax.axis_size(axis))
    route = [(i - distance, i) for i in devices if i - distance in devices]
    return lax.ppermute(block, axis, route)


def shards(
    positions, right_sides, leaf_basis, leaf_transfer, far_coupling, top_transfer, top_coupling,
    near_list, send_leaf, send_count, far_target,
):
    both = ("group", "dev")
    points = OWN * LEAF
    rim = EDGE * LEAF
    place = (lax.axis_index("group") * lax.axis_size("dev") + lax.axis_index("dev")).astype(jnp.int32).reshape(1)

    first, last = pl.pallas_call(
        pack_kernel,
        out_shape=(jax.ShapeDtypeStruct((2 * N, rim), BF16),) * 2,
        in_specs=[ANY, ANY],
        out_specs=(VMEM, VMEM),
        scratch_shapes=[pltpu.VMEM((3, points), F32), pltpu.VMEM((N, points), F32), pltpu.SemaphoreType.DMA((8,))],
        compiler_params=params(60),
        cost_estimate=pl.CostEstimate(flops=10**7, bytes_accessed=3 << 20, transcendentals=0),
        name="pack",
    )(positions, right_sides)
    below = from_behind(last, both, 1)
    above = from_behind(first, both, -1)

    message = pl.pallas_call(
        moment_kernel,
        out_shape=jax.ShapeDtypeStruct((OWN * 4 * N, 2 * R), BF16),
        in_specs=[SMEM, SMEM, SMEM, ANY, ANY, ANY, ANY],
        out_specs=VMEM,
        scratch_shapes=[
            pltpu.VMEM((N, points), F32),
            pltpu.VMEM((OWN, R, LEAF), BF16),
            pltpu.VMEM((R, OWN * R), BF16),
            pltpu.VMEM((6, 8, R * R), F32),
            pltpu.VMEM((OWN, N, 2 * R), F32),
            pltpu.VMEM((7, N, 2 * R), F32),
            pltpu.VMEM((6, R, R), F32),
            pltpu.SemaphoreType.DMA((18,)),
        ],
        compiler_params=params(60),
        cost_estimate=pl.CostEstimate(flops=10**9, bytes_accessed=12 << 20, transcendentals=0),
        name="moments",
    )(place, send_leaf[0].T, send_count, right_sides, leaf_basis, leaf_transfer, top_transfer)
    incoming = lax.all_to_all(message, both, split_axis=0, concat_axis=0, tiled=True)

    near = pl.pallas_call(
        near_kernel,
        out_shape=jax.ShapeDtypeStruct((N, points), F32),
        in_specs=[SMEM] + [VMEM] * 4,
        out_specs=VMEM,
        scratch_shapes=[
            pltpu.VMEM((SEEN, LEAF, FEAT), BF16),
            pltpu.VMEM((OWN, FEAT, LEAF), BF16),
            pltpu.VMEM((SEEN, N, LEAF), F32),
        ],
        compiler_params=params(56),
        cost_estimate=pl.CostEstimate(flops=60 * 10**9, bytes_accessed=6 << 20, transcendentals=0),
        name="near",
    )(near_list.T, below, positions, right_sides, above)

    return pl.pallas_call(
        far_kernel,
        out_shape=jax.ShapeDtypeStruct((N, points), F32),
        in_specs=[SMEM, SMEM, VMEM, VMEM, ANY, ANY, ANY, ANY, ANY],
        out_specs=VMEM,
        scratch_shapes=[
            pltpu.VMEM((OWN, R, SLOTS * R), BF16),
            pltpu.VMEM((R, OWN * R), BF16),
            pltpu.VMEM((OWN, R, LEAF), BF16),
            pltpu.VMEM((6, 8, R * R), F32),
            pltpu.VMEM((6, 8, R * R), F32),
            pltpu.VMEM((OWN, N, R), F32),
            pltpu.VMEM((13, R, R), F32),
            pltpu.VMEM((8, N, 2 * R), F32),
            pltpu.SemaphoreType.DMA((18,)),
        ],
        compiler_params=params(56),
        cost_estimate=pl.CostEstimate(flops=2 * 10**9, bytes_accessed=22 << 20, transcendentals=0),
        name="far_field",
    )(place, far_target[0].T, incoming, near, far_coupling[0], leaf_transfer, leaf_basis, top_transfer, top_coupling)


def solution(mesh):
    both = ("group", "dev")
    placed = (
        P(None, both), P(None, both), P(both, None, None), P(None, both), P(both, None, None, None),
        P(), P(), P(both, None), P(both, None, None), P(both, None), P(both, None, None),
    )
    return jax.shard_map(shards, mesh=mesh, in_specs=placed, out_specs=P(None, both), check_vma=False)
```

time: 143 us -> 107 us (0.75)
  Pallas kernels: 112 us -> 85.1 us
  local copies, waits for them, and re-layouts: 13 us -> 3.91 us
    pallas_call x1, Pallas kernels: 78.5 us -> 58.4 us  [shards(): pl.pallas_call(near_kernel, out_shape=jax.ShapeDtypeStruct((N, points), F...]
    unnamed x24 -> x10, local copies, waits for them, and re-layouts: 13 us -> 3.91 us
    pallas_call x1, Pallas kernels: 20.2 us -> 14.5 us  [shards(): pl.pallas_call(far_kernel, out_shape=jax.ShapeDtypeStruct((N, points), F3...]
    pallas_call x1, Pallas kernels: 12.7 us -> 9.82 us  [shards(): pl.pallas_call(moment_kernel, out_shape=jax.ShapeDtypeStruct((OWN * 4 * N...]
    pallas_call x1, Pallas kernels: 0.68 us -> 2.43 us  [shards(): pl.pallas_call(pack_kernel, out_shape=(jax.ShapeDtypeStruct((2 * N, rim),...]
  transfers between devices with their start and end apart: 3 -> 3, of which waited for: 0 -> 0; matrix products, arithmetic and copies ran while one was open for 1% -> 2% of each run, Pallas kernels for 64% -> 65%
where the time goes in v3:
time: 107 us; the launch traced here: 105 us
  Pallas kernels  85.1 us (80%)
  starting transfers between devices  16.3 us (15%)
  local copies, waits for them, and re-layouts  3.91 us (4%)
    pallas_call x1, Pallas kernels, shards(): pl.pallas_call(near_kernel, out_shape=jax.ShapeDtypeStruct((N, points), F...  58.4 us
    pallas_call x1, Pallas kernels, shards(): pl.pallas_call(far_kernel, out_shape=jax.ShapeDtypeStruct((N, points), F3...  14.5 us
    all_to_all x1, starting transfers between devices, shards(): lax.all_to_all(message, both, split_axis=0, concat_axis=0, tiled=True)  10.5 us
    pallas_call x1, Pallas kernels, shards(): pl.pallas_call(moment_kernel, out_shape=jax.ShapeDtypeStruct((OWN * 4 * N...  9.82 us
    ppermute x2, starting transfers between devices, from_behind(): return lax.ppermute(block, axis, route)  5.84 us
    unnamed x10, local copies, waits for them, and re-layouts  3.91 us
    pallas_call x1, Pallas kernels, shards(): pl.pallas_call(pack_kernel, out_shape=(jax.ShapeDtypeStruct((2 * N, rim),...  2.43 us
  transfers between devices with their start and end apart: 3, of which 0 were waited for; matrix products, arithmetic and copies ran while one was open for 2% of the time, Pallas kernels for 65%

profile of v3, /device:TPU:4, one launch (start us, length us, event | category | flops | bytes accessed | tf_op | source)
XLA Modules:
  0.0 105.5 jit_solution(15353904624646605489)
XLA Ops:
  0.0 2.4 %pack.1 = (bf16[16,16384]{1,0:T(8,128)(2,1)}, bf16[16,16384]{1,0:T(8,128)(2,1)}) custom-call(f32[3,32768]{1,0:T(4,128)} %points.1, f32[8,32768]{1,0:T(8,128)} %values.1), custom_call_target="tpu_custom_call" | custom-call | flops 10000000 | bytes 3145728 | tf_op jit(solution)/shard_map/pack/pallas_call | solution.py:363
  2.4 3.1 %collective-permute-start = (bf16[16,16384]{1,0:T(8,128)(2,1)}, bf16[16,16384]{1,0:T(8,128)(2,1)S(1)}, u32[]{:S(2)}, u32[]{:S(2)}) collective-permute-start(bf16[16,16384]{1,0:T(8,128)(2,1)} %get-tuple-element.7), channel_id=1, source_target_pairs={{0,1},{1,2},{2,3},{3,4},{4,5},{5,6},{6,7},{7,8},{8,9},{9,10},{10,1... | collective-permute-start | bytes 1572872 | tf_op jit(solution)/shard_map/ppermute | solution.py:351
  5.6 2.7 %collective-permute-start.1 = (bf16[16,16384]{1,0:T(8,128)(2,1)}, bf16[16,16384]{1,0:T(8,128)(2,1)S(1)}, u32[]{:S(2)}, u32[]{:S(2)}) collective-permute-start(bf16[16,16384]{1,0:T(8,128)(2,1)} %get-tuple-element.8), channel_id=1, source_target_pairs={{1,0},{2,1},{3,2},{4,3},{5,4},{6,5},{7,6},{8,7},{9,8},{10,9},{11,1... | collective-permute-start | bytes 1572872 | tf_op jit(solution)/shard_map/ppermute | solution.py:351
  8.3 1.3 %copy.16 = s32[1,128,6]{1,2,0:T(8,128)} copy(s32[1,128,6]{1,0,2:T(1,128)} %param.19) | data formatting | bytes 6144
  9.6 0.0 copy-start.1
  9.6 9.8 %moments.1 = bf16[4096,128]{1,0:T(8,128)(2,1)} custom-call(s32[1]{0:T(128)} %bitcast.place, s32[6,128]{1,0:T(8,128)} %bitcast.18, s32[1,128]{1,0:T(1,128)} %send_count.1, f32[8,32768]{1,0:T(8,128)} %values.1, bf16[128,64,256]{2,1,0:T(8,128)(2,1)} %basis_hbm.3, bf16[64,8192]{1,0:T(8,128)(2,1)} %transfer_hbm.3, f32[254,4096]{1,0:T(8,128)} %top_transfer_hbm.3), custom_call_target="tpu_custom_call" | custom-call | flops 1000000000 | bytes 12582912 | tf_op jit(solution)/shard_map/moments/pallas_call | solution.py:376
  19.4 10.5 %all-to-all-start = ((bf16[128,32,128]{2,1,0:T(8,128)(2,1)}), bf16[128,32,128]{2,1,0:T(8,128)(2,1)S(1)}, u32[]{:S(2)}, u32[]{:S(2)}) async-start(bf16[128,32,128]{2,1,0:T(8,128)(2,1)} %bitcast.17), calls=%async_computation | async-start | bytes 2097152 | tf_op jit(solution)/shard_map/all_to_all | solution.py:395
  29.9 0.0 copy-done.1
  29.9 0.6 copy.17
  30.5 0.0 collective-permute-done.below
  30.5 0.0 copy-start.2
  30.5 0.0 collective-permute-done.1.above
  30.5 0.0 copy-start.3
  30.6 0.8 copy-done.2
  31.3 0.2 copy-done.3
  31.6 58.4 %near.1 = f32[8,32768]{1,0:T(8,128)} custom-call(s32[6,128]{1,0:T(8,128)} %bitcast.20, bf16[16,16384]{1,0:T(8,128)(2,1)} %copy-done.2, f32[3,32768]{1,0:T(4,128)} %points.1, f32[8,32768]{1,0:T(8,128)} %values.1, bf16[16,16384]{1,0:T(8,128)(2,1)} %copy-done.3), custom_call_target="tpu_custom_call" | custom-call | flops 60000002048 | bytes 6291456 | tf_op jit(solution)/shard_map/near/pallas_call | solution.py:397
  90.0 0.0 all-to-all-done
  90.0 0.0 copy-start
  90.0 1.0 copy-done
  91.0 14.5 %far_field.1 = f32[8,32768]{1,0:T(8,128)} custom-call(s32[1]{0:T(128)} %bitcast.place, s32[6,128]{1,0:T(8,128)} %bitcast.19, bf16[4096,128]{1,0:T(8,128)(2,1)} %bitcast.16, f32[8,32768]{1,0:T(8,128)} %near.1, bf16[128,64,384]{2,1,0:T(8,128)(2,1)} %bitcast.15, bf16[64,8192]{1,0:T(8,128)(2,1)} %transfer_hbm.3, bf16[128,64,256]{2,1,0:T(8,128)(2,1)} %basis_hbm.3, ...), custom_call_target="tpu_custom_call" | custom-call | flops 2000000000 | bytes 23068672 | tf_op jit(solution)/shard_map/far_field/pallas_call | solution.py:412
Async XLA Ops:
  2.4 28.1 %collective-permute-start = (bf16[16,16384]{1,0:T(8,128)(2,1)}, bf16[16,16384]{1,0:T(8,128)(2,1)S(1)}, u32[]{:S(2)}, u32[]{:S(2)}) collective-permute-start(bf16[16,16384]{1,0:T(8,128)(2,1)} %get-tuple-element.7), channel_id=1, source_target_pairs={{0,1},{1,2},{2,3},{3,4},{4,5},{5,6},{6,7},{7,8},{8,9},{9,10},{10,1... | collective-permute-start | bytes 1572872 | tf_op jit(solution)/shard_map/ppermute | solution.py:351
  5.6 25.0 %collective-permute-start.1 = (bf16[16,16384]{1,0:T(8,128)(2,1)}, bf16[16,16384]{1,0:T(8,128)(2,1)S(1)}, u32[]{:S(2)}, u32[]{:S(2)}) collective-permute-start(bf16[16,16384]{1,0:T(8,128)(2,1)} %get-tuple-element.8), channel_id=1, source_target_pairs={{1,0},{2,1},{3,2},{4,3},{5,4},{6,5},{7,6},{8,7},{9,8},{10,9},{11,1... | collective-permute-start | bytes 1572872 | tf_op jit(solution)/shard_map/ppermute | solution.py:351
  9.6 20.3 %copy-start.1 = (s32[1,128,6]{1,0,2:T(1,128)S(1)}, s32[1,128,6]{1,0,2:T(1,128)}, u32[]{:S(2)}) copy-start(s32[1,128,6]{1,0,2:T(1,128)} %param.21) | copy-start | bytes 9220
  19.4 70.6 %all-to-all-start = ((bf16[128,32,128]{2,1,0:T(8,128)(2,1)}), bf16[128,32,128]{2,1,0:T(8,128)(2,1)S(1)}, u32[]{:S(2)}, u32[]{:S(2)}) async-start(bf16[128,32,128]{2,1,0:T(8,128)(2,1)} %bitcast.17), calls=%async_computation | async-start | bytes 2097152 | tf_op jit(solution)/shard_map/all_to_all | solution.py:395
  30.5 0.8 copy-start.2
  30.5 1.0 copy-start.3
  90.0 1.0 copy-start

commit v4 on v3

--- a/solution.py
+++ b/solution.py
@@ -28,7 +28,7 @@
 NT = (((1,), (1,)), ((), ()))
 VMEM = pl.BlockSpec(memory_space=pltpu.VMEM)
 SMEM = pl.BlockSpec(memory_space=pltpu.SMEM)
-ANY = pl.BlockSpec(memory_space=pl.ANY)
+HBM = pl.BlockSpec(memory_space=pltpu.HBM)
 
 
 def dot(a, b, dims=NN):
@@ -95,24 +95,22 @@
     return lax.rsqrt(distance).astype(BF16)
 
 
-def pack_kernel(points_hbm, values_hbm, first, last, points, values, sems):
-    chunks = 4
-    width = OWN * LEAF // chunks
-    copies = []
-    for i in range(chunks):
-        some = pl.ds(i * width, width)
-        copies.append(pltpu.make_async_copy(points_hbm.at[:, some], points.at[:, some], sems.at[2 * i]))
-        copies.append(pltpu.make_async_copy(values_hbm.at[:, some], values.at[:, some], sems.at[2 * i + 1]))
+def pack_kernel(place, points_hbm, values_hbm, first, second, points, values, sems):
+    copies = [
+        pltpu.make_async_copy(points_hbm, points, sems.at[0]),
+        pltpu.make_async_copy(values_hbm, values, sems.at[1]),
+    ]
     for copy in copies:
         copy.start()
-    for i in range(chunks):
-        copies[2 * i].wait()
-        copies[2 * i + 1].wait()
-        for j in range(i * width, (i + 1) * width, 4 * LEAF):
-            some = slice(j, j + 4 * LEAF)
-            out, start = (first, j) if j < EDGE * LEAF else (last, j - EDGE * LEAF)
+    for copy in copies:
+        copy.wait()
+    odd = lax.bitwise_and(place[0], 1)
+    width = 4 * LEAF
+    for out, side in ((first, 1 - odd), (second, odd)):
+        for j in range(EDGE // 4):
+            some = aligned(side * (EDGE // 4) + j, width)
             rows = jnp.concatenate([values[:, some], split_points(points[:, some])], 0)
-            out[:, start : start + 4 * LEAF] = rows.astype(BF16)
+            out[:, j * width : (j + 1) * width] = rows.astype(BF16)
 
 
 def top_bit(x):
@@ -195,8 +193,8 @@
         parts = []
         count = send_count[0, p]
         for pair in range(SLOTS // 2):
-            left = moments[send_leaf[2 * pair, p]]
-            right = moments[send_leaf[2 * pair + 1, p]]
+            left = moments[send_leaf[2 * pair, 0, p]]
+            right = moments[send_leaf[2 * pair + 1, 0, p]]
             left = jnp.where(2 * pair < count, left, 0.0)
             right = jnp.where(2 * pair + 1 < count, right, 0.0)
             parts.append(jnp.where(is_left, left, right))
@@ -208,13 +206,21 @@
 
 
 def near_kernel(
-    near_list, below, points, values, above, out, sources, targets, seen_values,
+    place, near_list, first, second, points_hbm, values_hbm, out, points, values, sources, targets, seen_values, sems,
 ):
-    def rim(ref, first):
+    copies = [
+        pltpu.make_async_copy(points_hbm, points, sems.at[0]),
+        pltpu.make_async_copy(values_hbm, values, sems.at[1]),
+    ]
+    for copy in copies:
+        copy.start()
+    odd = lax.bitwise_and(place[0], 1)
+
+    def rim(ref, start):
         def one(i, carry):
             block = ref[:, aligned(i, LEAF)].astype(F32)
-            sources[first + i] = source_features(block[N:, :])
-            seen_values[first + i] = block[:N, :]
+            sources[start + i] = source_features(block[N:, :])
+            seen_values[start + i] = block[:N, :]
             return carry
 
         lax.fori_loop(0, EDGE, one, 0, unroll=4)
@@ -226,27 +232,30 @@
         seen_values[EDGE + i] = values[:, aligned(i, LEAF)]
         return carry
 
+    rim(first, (1 - odd) * (EDGE + OWN))
+    rim(second, odd * (EDGE + OWN))
+    for copy in copies:
+        copy.wait()
     lax.fori_loop(0, OWN, own, 0, unroll=4)
-    rim(below, 0)
-    rim(above, EDGE + OWN)
-
-    def finish(leaf, seen, kernels):
-        total = dot(seen_values[seen[0]].astype(BF16), kernels[0])
-        for e, kernel in zip(seen[1:], kernels[1:]):
-            total = total + dot(seen_values[e].astype(BF16), kernel)
-        out[:, aligned(leaf, LEAF)] = total
 
     def eight_leaves(g, carry):
-        waiting = None
+        pairs = []
         for j in range(8):
             leaf = g * 8 + j
-            target = targets[leaf]
             seen = [EDGE + leaf] + [near_list[k, leaf] for k in range(NEAR)]
-            kernels = [inverse_root(dot(sources[e], target)) for e in seen]
-            if waiting is not None:
-                finish(*waiting)
-            waiting = (leaf, seen, kernels)
-        finish(*waiting)
+            pairs.extend((leaf, (j, k), e) for k, e in enumerate(seen))
+        groups = [pairs[i : i + 8] for i in range(0, len(pairs), 8)]
+        kernels = {}
+        total = None
+        for ahead, now in zip(groups + [[]], [[]] + groups):
+            for i in range(0, 8, 4):
+                for leaf, pair, e in ahead[i : i + 4]:
+                    kernels[pair] = inverse_root(dot(sources[e], targets[leaf]))
+                for leaf, pair, e in now[i : i + 4]:
+                    part = dot(seen_values[e].astype(BF16), kernels.pop(pair))
+                    total = part if pair[1] == 0 else total + part
+                    if pair[1] == NEAR:
+                        out[:, aligned(leaf, LEAF)] = total
         return carry
 
     lax.fori_loop(0, OWN // 8, eight_leaves, 0)
@@ -261,22 +270,26 @@
 
 
 def far_kernel(
-    place, far_target, incoming, near,
+    place, far_target, incoming, near_hbm,
     coupling_hbm, transfer_hbm, basis_hbm, top_transfer_hbm, top_coupling_hbm,
-    out,
-    coupling, transfer, basis, transfer_rows, coupling_rows, far_local, matrices, siblings, sems,
+    out_hbm,
+    near, out, coupling, transfer, basis, transfer_rows, coupling_rows, far_local, matrices, siblings, sems,
 ):
     owner = place[0]
     chunks = 4
     chunk = OWN // chunks
     copies = []
     for i in range(chunks):
-        copies.append(pltpu.make_async_copy(coupling_hbm.at[pl.ds(i * chunk, chunk)], coupling.at[pl.ds(i * chunk, chunk)], sems.at[i]))
-    copies.append(pltpu.make_async_copy(transfer_hbm, transfer, sems.at[chunks]))
-    copies.append(pltpu.make_async_copy(basis_hbm, basis, sems.at[chunks + 1]))
-    paths = path_copies(top_transfer_hbm, transfer_rows, owner, sems, chunks + 2)
-    paths = paths + path_copies(top_coupling_hbm, coupling_rows, owner, sems, chunks + 8)
-    for copy in copies[:chunks] + paths + copies[chunks:]:
+        some = pl.ds(i * chunk, chunk)
+        copies.append(pltpu.make_async_copy(coupling_hbm.at[some], coupling.at[some], sems.at[i]))
+    paths = path_copies(top_transfer_hbm, transfer_rows, owner, sems, chunks)
+    paths = paths + path_copies(top_coupling_hbm, coupling_rows, owner, sems, chunks + 6)
+    first = chunks + 12
+    rest = [
+        pltpu.make_async_copy(source, target, sems.at[first + i])
+        for i, (source, target) in enumerate([(transfer_hbm, transfer), (basis_hbm, basis), (near_hbm, near)])
+    ]
+    for copy in copies + paths + rest:
         copy.start()
 
     far_local[...] = jnp.zeros_like(far_local)
@@ -303,7 +316,7 @@
                 level = jnp.where(p == owner, 7, top_bit(owner ^ p))
                 siblings[level] = siblings[level] + arrived[(j * 4 + 3) * N : (j * 4 + 4) * N, :]
                 for slot in range(SLOTS):
-                    leaf = far_target[slot, p]
+                    leaf = far_target[slot, 0, p]
                     part = results[j * 3 + slot // 2][(slot % 2) * N : (slot % 2 + 1) * N, :]
                     far_local[leaf] = far_local[leaf] + part
             return carry
@@ -329,8 +342,8 @@
     row_leaf = lax.broadcasted_iota(jnp.int32, (4 * N, 4 * R), 0) // N
     column_leaf = lax.broadcasted_iota(jnp.int32, (4 * N, 4 * R), 1) // R
     fields = jnp.where(row_leaf == column_leaf, wide, 0.0).astype(BF16)
-    copies[chunks].wait()
-    copies[chunks + 1].wait()
+    for copy in rest:
+        copy.wait()
 
     def some_leaves(g, carry):
         locals_ = []
@@ -342,13 +355,19 @@
             out[:, aligned(leaf, LEAF)] = near[:, aligned(leaf, LEAF)] + dot(total, basis[leaf])
         return carry
 
-    lax.fori_loop(0, OWN // 16, some_leaves, 0)
-
-
-def from_behind(block, axis, distance):
-    devices = range(lax.axis_size(axis))
-    route = [(i - distance, i) for i in devices if i - distance in devices]
-    return lax.ppermute(block, axis, route)
+    results = []
+    for i in range(chunks):
+        lax.fori_loop(i * chunk // 16, (i + 1) * chunk // 16, some_leaves, 0)
+        some = pl.ds(i * chunk * LEAF, chunk * LEAF)
+        results.append(pltpu.make_async_copy(out.at[:, some], out_hbm.at[:, some], sems.at[first + 3 + i]))
+        results[-1].start()
+    for copy in results:
+        copy.wait()
+
+
+def swapped(block, axis, start):
+    lower = range(start, lax.axis_size(axis) - 1, 2)
+    return lax.ppermute(block, axis, [(i, i + 1) for i in lower] + [(i + 1, i) for i in lower])
 
 
 def shards(
@@ -360,23 +379,23 @@
     rim = EDGE * LEAF
     place = (lax.axis_index("group") * lax.axis_size("dev") + lax.axis_index("dev")).astype(jnp.int32).reshape(1)
 
-    first, last = pl.pallas_call(
+    first, second = pl.pallas_call(
         pack_kernel,
         out_shape=(jax.ShapeDtypeStruct((2 * N, rim), BF16),) * 2,
-        in_specs=[ANY, ANY],
+        in_specs=[SMEM, HBM, HBM],
         out_specs=(VMEM, VMEM),
-        scratch_shapes=[pltpu.VMEM((3, points), F32), pltpu.VMEM((N, points), F32), pltpu.SemaphoreType.DMA((8,))],
-        compiler_params=params(60),
+        scratch_shapes=[pltpu.VMEM((3, points), F32), pltpu.VMEM((N, points), F32), pltpu.SemaphoreType.DMA((2,))],
+        compiler_params=params(63),
         cost_estimate=pl.CostEstimate(flops=10**7, bytes_accessed=3 << 20, transcendentals=0),
         name="pack",
-    )(positions, right_sides)
-    below = from_behind(last, both, 1)
-    above = from_behind(first, both, -1)
+    )(place, positions, right_sides)
+    first = swapped(first, both, 0)
+    second = swapped(second, both, 1)
 
     message = pl.pallas_call(
         moment_kernel,
         out_shape=jax.ShapeDtypeStruct((OWN * 4 * N, 2 * R), BF16),
-        in_specs=[SMEM, SMEM, SMEM, ANY, ANY, ANY, ANY],
+        in_specs=[SMEM, SMEM, SMEM, HBM, HBM, HBM, HBM],
         out_specs=VMEM,
         scratch_shapes=[
             pltpu.VMEM((N, points), F32),
@@ -388,33 +407,38 @@
             pltpu.VMEM((6, R, R), F32),
             pltpu.SemaphoreType.DMA((18,)),
         ],
-        compiler_params=params(60),
+        compiler_params=params(63),
         cost_estimate=pl.CostEstimate(flops=10**9, bytes_accessed=12 << 20, transcendentals=0),
         name="moments",
-    )(place, send_leaf[0].T, send_count, right_sides, leaf_basis, leaf_transfer, top_transfer)
+    )(place, send_leaf.transpose(2, 0, 1), send_count, right_sides, leaf_basis, leaf_transfer, top_transfer)
     incoming = lax.all_to_all(message, both, split_axis=0, concat_axis=0, tiled=True)
 
     near = pl.pallas_call(
         near_kernel,
         out_shape=jax.ShapeDtypeStruct((N, points), F32),
-        in_specs=[SMEM] + [VMEM] * 4,
+        in_specs=[SMEM, SMEM, VMEM, VMEM, HBM, HBM],
         out_specs=VMEM,
         scratch_shapes=[
+            pltpu.VMEM((3, points), F32),
+            pltpu.VMEM((N, points), F32),
             pltpu.VMEM((SEEN, LEAF, FEAT), BF16),
             pltpu.VMEM((OWN, FEAT, LEAF), BF16),
             pltpu.VMEM((SEEN, N, LEAF), F32),
+            pltpu.SemaphoreType.DMA((2,)),
         ],
-        compiler_params=params(56),
+        compiler_params=params(63),
         cost_estimate=pl.CostEstimate(flops=60 * 10**9, bytes_accessed=6 << 20, transcendentals=0),
         name="near",
-    )(near_list.T, below, positions, right_sides, above)
+    )(place, near_list.T, first, second, positions, right_sides)
 
     return pl.pallas_call(
         far_kernel,
         out_shape=jax.ShapeDtypeStruct((N, points), F32),
-        in_specs=[SMEM, SMEM, VMEM, VMEM, ANY, ANY, ANY, ANY, ANY],
-        out_specs=VMEM,
+        in_specs=[SMEM, SMEM, VMEM] + [HBM] * 6,
+        out_specs=HBM,
         scratch_shapes=[
+            pltpu.VMEM((N, points), F32),
+            pltpu.VMEM((N, points), F32),
             pltpu.VMEM((OWN, R, SLOTS * R), BF16),
             pltpu.VMEM((R, OWN * R), BF16),
             pltpu.VMEM((OWN, R, LEAF), BF16),
@@ -423,12 +447,12 @@
             pltpu.VMEM((OWN, N, R), F32),
             pltpu.VMEM((13, R, R), F32),
             pltpu.VMEM((8, N, 2 * R), F32),
-            pltpu.SemaphoreType.DMA((18,)),
+            pltpu.SemaphoreType.DMA((23,)),
         ],
-        compiler_params=params(56),
+        compiler_params=params(63),
         cost_estimate=pl.CostEstimate(flops=2 * 10**9, bytes_accessed=22 << 20, transcendentals=0),
         name="far_field",
-    )(place, far_target[0].T, incoming, near, far_coupling[0], leaf_transfer, leaf_basis, top_transfer, top_coupling)
+    )(place, far_target.transpose(2, 0, 1), incoming, near, far_coupling[0], leaf_transfer, leaf_basis, top_transfer, top_coupling)
 
 
 def solution(mesh):

time: 107 us -> 99.7 us (0.932)
  local copies, waits for them, and re-layouts: 3.91 us -> 0.78 us
  Pallas kernels: 85.1 us -> 82.2 us
    unnamed x10 -> x2, local copies, waits for them, and re-layouts: 3.91 us -> 0.78 us
    ppermute x2, starting transfers between devices: 5.84 us -> 3.19 us  [swapped(): lax.ppermute(block, axis, [(i, i + 1) for i in lower] + [(i + 1, i) for i...]
    pallas_call x1, Pallas kernels: 58.4 us -> 55.9 us  [shards(): pl.pallas_call(near_kernel, out_shape=jax.ShapeDtypeStruct((N, points), F...]
    all_to_all x1, starting transfers between devices: 10.5 us -> 12.2 us  [shards(): lax.all_to_all(message, both, split_axis=0, concat_axis=0, tiled=True)]
  transfers between devices with their start and end apart: 3 -> 3, of which waited for: 0 -> 0; matrix products, arithmetic and copies ran while one was open for 2% -> 0% of each run, Pallas kernels for 65% -> 67%
where the time goes in v4:
time: 99.7 us; the launch traced here: 98.4 us
  Pallas kernels  82.2 us (82%)
  starting transfers between devices  15.4 us (15%)
    pallas_call x1, Pallas kernels, shards(): pl.pallas_call(near_kernel, out_shape=jax.ShapeDtypeStruct((N, points), F...  55.9 us
    pallas_call x1, Pallas kernels, shards(): pl.pallas_call(far_kernel, out_shape=jax.ShapeDtypeStruct((N, points), F3...  13.9 us
    all_to_all x1, starting transfers between devices, shards(): lax.all_to_all(message, both, split_axis=0, concat_axis=0, tiled=True)  12.2 us
    pallas_call x1, Pallas kernels, shards(): pl.pallas_call(moment_kernel, out_shape=jax.ShapeDtypeStruct((OWN * 4 * N...  9.68 us
    ppermute x2, starting transfers between devices, swapped(): lax.ppermute(block, axis, [(i, i + 1) for i in lower] + [(i + 1, i) for i...  3.19 us
    pallas_call x1, Pallas kernels, shards(): pl.pallas_call(pack_kernel, out_shape=(jax.ShapeDtypeStruct((2 * N, rim),...  2.72 us
  transfers between devices with their start and end apart: 3, of which 0 were waited for; matrix products, arithmetic and copies ran while one was open for 0% of the time, Pallas kernels for 67%

profile of v4, /device:TPU:4, one launch (start us, length us, event | category | flops | bytes accessed | tf_op | source)
XLA Modules:
  0.0 98.4 jit_solution(2288571904868897908)
XLA Ops:
  0.0 2.7 %pack.1 = (bf16[16,16384]{1,0:T(8,128)(2,1)}, bf16[16,16384]{1,0:T(8,128)(2,1)}) custom-call(s32[1]{0:T(128)} %bitcast.place, f32[3,32768]{1,0:T(4,128)} %points_hbm.3, f32[8,32768]{1,0:T(8,128)} %values_hbm.5), custom_call_target="tpu_custom_call" | custom-call | flops 10000000 | bytes 3145728 | tf_op jit(solution)/shard_map/pack/pallas_call | solution.py:382
  2.7 1.3 %collective-permute-start = (bf16[16,16384]{1,0:T(8,128)(2,1)}, bf16[16,16384]{1,0:T(8,128)(2,1)S(1)}, u32[]{:S(2)}, u32[]{:S(2)}) collective-permute-start(bf16[16,16384]{1,0:T(8,128)(2,1)} %get-tuple-element.7), channel_id=1, source_target_pairs={{0,1},{2,3},{4,5},{6,7},{8,9},{10,11},{12,13},{14,15},{16,17},{18,... | collective-permute-start | bytes 1572872 | tf_op jit(solution)/shard_map/ppermute | solution.py:370
  4.0 1.9 %collective-permute-start.1 = (bf16[16,16384]{1,0:T(8,128)(2,1)}, bf16[16,16384]{1,0:T(8,128)(2,1)}, u32[]{:S(2)}, u32[]{:S(2)}) collective-permute-start(bf16[16,16384]{1,0:T(8,128)(2,1)} %get-tuple-element.8), channel_id=1, source_target_pairs={{1,2},{3,4},{5,6},{7,8},{9,10},{11,12},{13,14},{15,16},{17,18},{19... | collective-permute-start | bytes 1572872 | tf_op jit(solution)/shard_map/ppermute | solution.py:370
  5.9 9.7 %moments.1 = bf16[4096,128]{1,0:T(8,128)(2,1)} custom-call(s32[1]{0:T(128)} %bitcast.place, s32[6,1,128]{2,1,0:T(1,128)} %bitcast.9, s32[1,128]{1,0:T(1,128)} %send_count.1, f32[8,32768]{1,0:T(8,128)} %values_hbm.5, bf16[128,64,256]{2,1,0:T(8,128)(2,1)} %basis_hbm.3, bf16[64,8192]{1,0:T(8,128)(2,1)} %transfer_hbm.3, f32[254,4096]{1,0:T(8,128)} %top_transfer_hbm.3), custom_call_target="tpu_custom_call" | custom-call | flops 1000000000 | bytes 12582912 | tf_op jit(solution)/shard_map/moments/pallas_call | solution.py:395
  15.6 12.2 %all-to-all-start = ((bf16[128,32,128]{2,1,0:T(8,128)(2,1)}), bf16[128,32,128]{2,1,0:T(8,128)(2,1)}, u32[]{:S(2)}, u32[]{:S(2)}) async-start(bf16[128,32,128]{2,1,0:T(8,128)(2,1)} %bitcast.8), calls=%async_computation | async-start | bytes 2097152 | tf_op jit(solution)/shard_map/all_to_all | solution.py:414
  27.8 0.0 collective-permute-done.first
  27.8 0.0 copy-start
  27.8 0.0 collective-permute-done.1.second
  27.8 0.8 copy-done
  28.6 55.9 %near.1.near_hbm = f32[8,32768]{1,0:T(8,128)} custom-call(s32[1]{0:T(128)} %bitcast.place, s32[6,128]{1,0:T(8,128)} %bitcast.11, bf16[16,16384]{1,0:T(8,128)(2,1)} %copy-done, bf16[16,16384]{1,0:T(8,128)(2,1)} %collective-permute-done.1.second, f32[3,32768]{1,0:T(4,128)} %points_hbm.3, f32[8,32768]{1,0:T(8,128)} %values_hbm.5), custom_call_target="tpu_custom_call" | custom-call | flops 60000002048 | bytes 6291456 | tf_op jit(solution)/shard_map/near/pallas_call | solution.py:416
  84.5 0.0 all-to-all-done
  84.5 13.9 %far_field.1 = f32[8,32768]{1,0:T(8,128)} custom-call(s32[1]{0:T(128)} %bitcast.place, s32[6,1,128]{2,1,0:T(1,128)} %bitcast.10, bf16[4096,128]{1,0:T(8,128)(2,1)} %bitcast.4.incoming, f32[8,32768]{1,0:T(8,128)} %near.1.near_hbm, bf16[128,64,384]{2,1,0:T(8,128)(2,1)} %bitcast.7, bf16[64,8192]{1,0:T(8,128)(2,1)} %transfer_hbm.3, ...), custom_call_target="tpu_custom_call" | custom-call | flops 2000000000 | bytes 23068672 | tf_op jit(solution)/shard_map/far_field/pallas_call | solution.py:434
Async XLA Ops:
  2.7 25.1 %collective-permute-start = (bf16[16,16384]{1,0:T(8,128)(2,1)}, bf16[16,16384]{1,0:T(8,128)(2,1)S(1)}, u32[]{:S(2)}, u32[]{:S(2)}) collective-permute-start(bf16[16,16384]{1,0:T(8,128)(2,1)} %get-tuple-element.7), channel_id=1, source_target_pairs={{0,1},{2,3},{4,5},{6,7},{8,9},{10,11},{12,13},{14,15},{16,17},{18,... | collective-permute-start | bytes 1572872 | tf_op jit(solution)/shard_map/ppermute | solution.py:370
  4.0 23.8 %collective-permute-start.1 = (bf16[16,16384]{1,0:T(8,128)(2,1)}, bf16[16,16384]{1,0:T(8,128)(2,1)}, u32[]{:S(2)}, u32[]{:S(2)}) collective-permute-start(bf16[16,16384]{1,0:T(8,128)(2,1)} %get-tuple-element.8), channel_id=1, source_target_pairs={{1,2},{3,4},{5,6},{7,8},{9,10},{11,12},{13,14},{15,16},{17,18},{19... | collective-permute-start | bytes 1572872 | tf_op jit(solution)/shard_map/ppermute | solution.py:370
  15.6 68.9 %all-to-all-start = ((bf16[128,32,128]{2,1,0:T(8,128)(2,1)}), bf16[128,32,128]{2,1,0:T(8,128)(2,1)}, u32[]{:S(2)}, u32[]{:S(2)}) async-start(bf16[128,32,128]{2,1,0:T(8,128)(2,1)} %bitcast.8), calls=%async_computation | async-start | bytes 2097152 | tf_op jit(solution)/shard_map/all_to_all | solution.py:414
  27.8 0.8 copy-start

commit v5 on v4

--- a/solution.py
+++ b/solution.py
@@ -3,6 +3,7 @@
 
 import jax
 import jax.numpy as jnp
+import numpy as np
 from jax import lax
 from jax.experimental import pallas as pl
 from jax.experimental.pallas import tpu as pltpu
@@ -60,35 +61,31 @@
     return high + pltpu.roll(round16(x - high), 3, 0)
 
 
-def square_parts(parts, swapped, offset):
+def features(parts):
     row = lax.broadcasted_iota(jnp.int32, parts.shape, 0)
+    swapped = jnp.where(row < 3, pltpu.roll(parts, 5, 0), pltpu.roll(parts, 3, 0))
     x = jnp.where(row < 3, parts + swapped, 0.0)
-    square = jnp.broadcast_to(jnp.sum(x * x, axis=0, keepdims=True), parts.shape) + offset
+    square = x * x
+    for shift in (4, 2, 1):
+        square = square + pltpu.roll(square, shift, 0)
     s0 = round16(square)
-    s1 = round16(square - s0)
-    return row, s0, s1, square - s0 - s1
-
-
-def swap_parts(parts):
-    row = lax.broadcasted_iota(jnp.int32, parts.shape, 0)
-    return jnp.where(row < 3, pltpu.roll(parts, 5, 0), pltpu.roll(parts, 3, 0))
-
-
-def source_features(parts):
-    row, s0, s1, s2 = square_parts(parts, swap_parts(parts), 0.0)
-    first = jnp.where(row < 6, parts, 1.0)
-    second = jnp.where(row < 6, parts, jnp.where(row == 6, s0, s1))
-    third = jnp.where(row == 0, 1.0, jnp.where(row == 1, s2, 0.0))
-    return jnp.concatenate([first, second, third, jnp.zeros_like(parts)], 0).astype(BF16).T
-
-
-def target_features(parts):
-    swapped = swap_parts(parts)
-    row, s0, s1, s2 = square_parts(parts, swapped, smoothing * inverse_scale * inverse_scale)
-    first = jnp.where(row < 6, -2.0 * parts, jnp.where(row == 6, s0, s1))
-    second = jnp.where(row < 6, -2.0 * swapped, 1.0)
-    third = jnp.where(row == 0, s2, jnp.where(row == 1, 1.0, 0.0))
-    return jnp.concatenate([first, second, third, jnp.zeros_like(parts)], 0).astype(BF16)
+    rest = square - s0
+    s1 = round16(rest)
+    s2 = rest - s1
+    squares = jnp.where(row == 6, s0, s1)
+    zero = jnp.zeros_like(parts)
+    offset = smoothing * inverse_scale * inverse_scale
+    offset_high = float(np.float32(np.asarray(offset, BF16)))
+    ones = jnp.where((row == 0) | (row == 2) | (row == 3), 1.0, 0.0)
+    offsets = jnp.where(row == 1, 1.0, jnp.where(row == 2, offset_high, jnp.where(row == 3, offset - offset_high, 0.0)))
+    source = [jnp.where(row < 6, parts, 1.0), jnp.where(row < 6, parts, squares), jnp.where(row == 1, s2, ones), zero]
+    target = [
+        jnp.where(row < 6, -2.0 * parts, squares),
+        jnp.where(row < 6, -2.0 * swapped, 1.0),
+        jnp.where(row == 0, s2, offsets),
+        zero,
+    ]
+    return jnp.concatenate(source, 0).astype(BF16).T, jnp.concatenate(target, 0).astype(BF16)
 
 
 def inverse_root(distance):
@@ -140,7 +137,7 @@
     message, values, basis, transfer, rows, moments, chain, matrices, sems,
 ):
     owner = place[0]
-    chunks = 4
+    chunks = 8
     chunk = OWN // chunks
     copies = []
     for i in range(chunks):
@@ -219,16 +216,15 @@
     def rim(ref, start):
         def one(i, carry):
             block = ref[:, aligned(i, LEAF)].astype(F32)
-            sources[start + i] = source_features(block[N:, :])
+            sources[start + i] = features(block[N:, :])[0]
             seen_values[start + i] = block[:N, :]
             return carry
 
-        lax.fori_loop(0, EDGE, one, 0, unroll=4)
+        lax.fori_loop(0, EDGE, one, 0, unroll=16)
 
     def own(i, carry):
         parts = split_points(points[:, aligned(i, LEAF)])
-        sources[EDGE + i] = source_features(parts)
-        targets[i] = target_features(parts)
+        sources[EDGE + i], targets[i] = features(parts)
         seen_values[EDGE + i] = values[:, aligned(i, LEAF)]
         return carry
 
@@ -236,12 +232,12 @@
     rim(second, odd * (EDGE + OWN))
     for copy in copies:
         copy.wait()
-    lax.fori_loop(0, OWN, own, 0, unroll=4)
-
-    def eight_leaves(g, carry):
+    lax.fori_loop(0, OWN, own, 0, unroll=16)
+
+    def sixteen_leaves(g, carry):
         pairs = []
-        for j in range(8):
-            leaf = g * 8 + j
+        for j in range(16):
+            leaf = g * 16 + j
             seen = [EDGE + leaf] + [near_list[k, leaf] for k in range(NEAR)]
             pairs.extend((leaf, (j, k), e) for k, e in enumerate(seen))
         groups = [pairs[i : i + 8] for i in range(0, len(pairs), 8)]
@@ -258,7 +254,7 @@
                         out[:, aligned(leaf, LEAF)] = total
         return carry
 
-    lax.fori_loop(0, OWN // 8, eight_leaves, 0)
+    lax.fori_loop(0, OWN // 16, sixteen_leaves, 0)
 
 
 def fetch(table, row, matrices, slot):
@@ -276,7 +272,7 @@
     near, out, coupling, transfer, basis, transfer_rows, coupling_rows, far_local, matrices, siblings, sems,
 ):
     owner = place[0]
-    chunks = 4
+    chunks = 8
     chunk = OWN // chunks
     copies = []
     for i in range(chunks):
@@ -321,7 +317,7 @@
                     far_local[leaf] = far_local[leaf] + part
             return carry
 
-        lax.fori_loop(i * chunk // 2, (i + 1) * chunk // 2, two_senders, 0, unroll=4)
+        lax.fori_loop(i * chunk // 2, (i + 1) * chunk // 2, two_senders, 0, unroll=8)
 
     for copy in paths:
         copy.wait()
@@ -405,7 +401,7 @@
             pltpu.VMEM((OWN, N, 2 * R), F32),
             pltpu.VMEM((7, N, 2 * R), F32),
             pltpu.VMEM((6, R, R), F32),
-            pltpu.SemaphoreType.DMA((18,)),
+            pltpu.SemaphoreType.DMA((30,)),
         ],
         compiler_params=params(63),
         cost_estimate=pl.CostEstimate(flops=10**9, bytes_accessed=12 << 20, transcendentals=0),
@@ -447,7 +443,7 @@
             pltpu.VMEM((OWN, N, R), F32),
             pltpu.VMEM((13, R, R), F32),
             pltpu.VMEM((8, N, 2 * R), F32),
-            pltpu.SemaphoreType.DMA((23,)),
+            pltpu.SemaphoreType.DMA((31,)),
         ],
         compiler_params=params(63),
         cost_estimate=pl.CostEstimate(flops=2 * 10**9, bytes_accessed=22 << 20, transcendentals=0),

time: 99.7 us -> 92.6 us (0.929)
  Pallas kernels: 82.2 us -> 74.9 us
    pallas_call x1, Pallas kernels: 55.9 us -> 50.5 us  [shards(): pl.pallas_call(near_kernel, out_shape=jax.ShapeDtypeStruct((N, points), F...]
    pallas_call x1, Pallas kernels: 13.9 us -> 12.2 us  [shards(): pl.pallas_call(far_kernel, out_shape=jax.ShapeDtypeStruct((N, points), F3...]
  transfers between devices with their start and end apart: 3 -> 3, of which waited for: 0 -> 0; matrix products, arithmetic and copies ran while one was open for 0% -> 0% of each run, Pallas kernels for 67% -> 66%
where the time goes in v5:
time: 92.6 us; the launch traced here: 91.3 us
  Pallas kernels  74.9 us (81%)
  starting transfers between devices  15.4 us (17%)
    pallas_call x1, Pallas kernels, shards(): pl.pallas_call(near_kernel, out_shape=jax.ShapeDtypeStruct((N, points), F...  50.5 us
    pallas_call x1, Pallas kernels, shards(): pl.pallas_call(far_kernel, out_shape=jax.ShapeDtypeStruct((N, points), F3...  12.2 us
    all_to_all x1, starting transfers between devices, shards(): lax.all_to_all(message, both, split_axis=0, concat_axis=0, tiled=True)  12.2 us
    pallas_call x1, Pallas kernels, shards(): pl.pallas_call(moment_kernel, out_shape=jax.ShapeDtypeStruct((OWN * 4 * N...  9.44 us
    ppermute x2, starting transfers between devices, swapped(): lax.ppermute(block, axis, [(i, i + 1) for i in lower] + [(i + 1, i) for i...  3.19 us
    pallas_call x1, Pallas kernels, shards(): pl.pallas_call(pack_kernel, out_shape=(jax.ShapeDtypeStruct((2 * N, rim),...  2.72 us
  transfers between devices with their start and end apart: 3, of which 0 were waited for; matrix products, arithmetic and copies ran while one was open for 0% of the time, Pallas kernels for 66%

profile of v5, /device:TPU:4, one launch (start us, length us, event | category | flops | bytes accessed | tf_op | source)
XLA Modules:
  0.0 91.3 jit_solution(1756791011203515620)
XLA Ops:
  0.0 2.7 %pack.1 = (bf16[16,16384]{1,0:T(8,128)(2,1)}, bf16[16,16384]{1,0:T(8,128)(2,1)}) custom-call(s32[1]{0:T(128)} %bitcast.place, f32[3,32768]{1,0:T(4,128)} %points_hbm.3, f32[8,32768]{1,0:T(8,128)} %values_hbm.5), custom_call_target="tpu_custom_call" | custom-call | flops 10000000 | bytes 3145728 | tf_op jit(solution)/shard_map/pack/pallas_call | solution.py:378
  2.7 1.3 %collective-permute-start = (bf16[16,16384]{1,0:T(8,128)(2,1)}, bf16[16,16384]{1,0:T(8,128)(2,1)S(1)}, u32[]{:S(2)}, u32[]{:S(2)}) collective-permute-start(bf16[16,16384]{1,0:T(8,128)(2,1)} %get-tuple-element.7), channel_id=1, source_target_pairs={{0,1},{2,3},{4,5},{6,7},{8,9},{10,11},{12,13},{14,15},{16,17},{18,... | collective-permute-start | bytes 1572872 | tf_op jit(solution)/shard_map/ppermute | solution.py:366
  4.0 1.9 %collective-permute-start.1 = (bf16[16,16384]{1,0:T(8,128)(2,1)}, bf16[16,16384]{1,0:T(8,128)(2,1)}, u32[]{:S(2)}, u32[]{:S(2)}) collective-permute-start(bf16[16,16384]{1,0:T(8,128)(2,1)} %get-tuple-element.8), channel_id=1, source_target_pairs={{1,2},{3,4},{5,6},{7,8},{9,10},{11,12},{13,14},{15,16},{17,18},{19... | collective-permute-start | bytes 1572872 | tf_op jit(solution)/shard_map/ppermute | solution.py:366
  5.9 9.4 %moments.1 = bf16[4096,128]{1,0:T(8,128)(2,1)} custom-call(s32[1]{0:T(128)} %bitcast.place, s32[6,1,128]{2,1,0:T(1,128)} %bitcast.9, s32[1,128]{1,0:T(1,128)} %send_count.1, f32[8,32768]{1,0:T(8,128)} %values_hbm.5, bf16[128,64,256]{2,1,0:T(8,128)(2,1)} %basis_hbm.3, bf16[64,8192]{1,0:T(8,128)(2,1)} %transfer_hbm.3, f32[254,4096]{1,0:T(8,128)} %top_transfer_hbm.3), custom_call_target="tpu_custom_call" | custom-call | flops 1000000000 | bytes 12582912 | tf_op jit(solution)/shard_map/moments/pallas_call | solution.py:391
  15.4 12.2 %all-to-all-start = ((bf16[128,32,128]{2,1,0:T(8,128)(2,1)}), bf16[128,32,128]{2,1,0:T(8,128)(2,1)}, u32[]{:S(2)}, u32[]{:S(2)}) async-start(bf16[128,32,128]{2,1,0:T(8,128)(2,1)} %bitcast.8), calls=%async_computation | async-start | bytes 2097152 | tf_op jit(solution)/shard_map/all_to_all | solution.py:410
  27.6 0.0 collective-permute-done.first
  27.6 0.0 copy-start
  27.6 0.0 collective-permute-done.1.second
  27.6 0.8 copy-done
  28.4 50.5 %near.1.near_hbm = f32[8,32768]{1,0:T(8,128)} custom-call(s32[1]{0:T(128)} %bitcast.place, s32[6,128]{1,0:T(8,128)} %bitcast.11, bf16[16,16384]{1,0:T(8,128)(2,1)} %copy-done, bf16[16,16384]{1,0:T(8,128)(2,1)} %collective-permute-done.1.second, f32[3,32768]{1,0:T(4,128)} %points_hbm.3, f32[8,32768]{1,0:T(8,128)} %values_hbm.5), custom_call_target="tpu_custom_call" | custom-call | flops 60000002048 | bytes 6291456 | tf_op jit(solution)/shard_map/near/pallas_call | solution.py:412
  78.9 0.0 all-to-all-done
  78.9 12.2 %far_field.1 = f32[8,32768]{1,0:T(8,128)} custom-call(s32[1]{0:T(128)} %bitcast.place, s32[6,1,128]{2,1,0:T(1,128)} %bitcast.10, bf16[4096,128]{1,0:T(8,128)(2,1)} %bitcast.4.incoming, f32[8,32768]{1,0:T(8,128)} %near.1.near_hbm, bf16[128,64,384]{2,1,0:T(8,128)(2,1)} %bitcast.7, bf16[64,8192]{1,0:T(8,128)(2,1)} %transfer_hbm.3, ...), custom_call_target="tpu_custom_call" | custom-call | flops 2000000000 | bytes 23068672 | tf_op jit(solution)/shard_map/far_field/pallas_call | solution.py:430
Async XLA Ops:
  2.7 24.8 %collective-permute-start = (bf16[16,16384]{1,0:T(8,128)(2,1)}, bf16[16,16384]{1,0:T(8,128)(2,1)S(1)}, u32[]{:S(2)}, u32[]{:S(2)}) collective-permute-start(bf16[16,16384]{1,0:T(8,128)(2,1)} %get-tuple-element.7), channel_id=1, source_target_pairs={{0,1},{2,3},{4,5},{6,7},{8,9},{10,11},{12,13},{14,15},{16,17},{18,... | collective-permute-start | bytes 1572872 | tf_op jit(solution)/shard_map/ppermute | solution.py:366
  4.0 23.6 %collective-permute-start.1 = (bf16[16,16384]{1,0:T(8,128)(2,1)}, bf16[16,16384]{1,0:T(8,128)(2,1)}, u32[]{:S(2)}, u32[]{:S(2)}) collective-permute-start(bf16[16,16384]{1,0:T(8,128)(2,1)} %get-tuple-element.8), channel_id=1, source_target_pairs={{1,2},{3,4},{5,6},{7,8},{9,10},{11,12},{13,14},{15,16},{17,18},{19... | collective-permute-start | bytes 1572872 | tf_op jit(solution)/shard_map/ppermute | solution.py:366
  15.4 63.6 %all-to-all-start = ((bf16[128,32,128]{2,1,0:T(8,128)(2,1)}), bf16[128,32,128]{2,1,0:T(8,128)(2,1)}, u32[]{:S(2)}, u32[]{:S(2)}) async-start(bf16[128,32,128]{2,1,0:T(8,128)(2,1)} %bitcast.8), calls=%async_computation | async-start | bytes 2097152 | tf_op jit(solution)/shard_map/all_to_all | solution.py:410
  27.6 0.8 copy-start

commit v6 on v5

--- a/solution.py
+++ b/solution.py
@@ -220,7 +220,7 @@
             seen_values[start + i] = block[:N, :]
             return carry
 
-        lax.fori_loop(0, EDGE, one, 0, unroll=16)
+        lax.fori_loop(0, EDGE, one, 0, unroll=32)
 
     def own(i, carry):
         parts = split_points(points[:, aligned(i, LEAF)])
@@ -232,12 +232,12 @@
     rim(second, odd * (EDGE + OWN))
     for copy in copies:
         copy.wait()
-    lax.fori_loop(0, OWN, own, 0, unroll=16)
-
-    def sixteen_leaves(g, carry):
+    lax.fori_loop(0, OWN, own, 0, unroll=32)
+
+    def many_leaves(g, carry):
         pairs = []
-        for j in range(16):
-            leaf = g * 16 + j
+        for j in range(32):
+            leaf = g * 32 + j
             seen = [EDGE + leaf] + [near_list[k, leaf] for k in range(NEAR)]
             pairs.extend((leaf, (j, k), e) for k, e in enumerate(seen))
         groups = [pairs[i : i + 8] for i in range(0, len(pairs), 8)]
@@ -254,7 +254,7 @@
                         out[:, aligned(leaf, LEAF)] = total
         return carry
 
-    lax.fori_loop(0, OWN // 16, sixteen_leaves, 0)
+    lax.fori_loop(0, OWN // 32, many_leaves, 0)
 
 
 def fetch(table, row, matrices, slot):

time: 92.6 us -> 91.1 us (0.984)
  Pallas kernels: 74.9 us -> 73.4 us
    pallas_call x1, Pallas kernels: 50.5 us -> 49 us  [shards(): pl.pallas_call(near_kernel, out_shape=jax.ShapeDtypeStruct((N, points), F...]
  transfers between devices with their start and end apart: 3 -> 3, of which waited for: 0 -> 0; matrix products, arithmetic and copies ran while one was open for 0% -> 0% of each run, Pallas kernels for 66% -> 65%
where the time goes in v6:
time: 91.1 us; the launch traced here: 89.8 us
  Pallas kernels  73.4 us (81%)
  starting transfers between devices  15.4 us (17%)
    pallas_call x1, Pallas kernels, shards(): pl.pallas_call(near_kernel, out_shape=jax.ShapeDtypeStruct((N, points), F...  49 us
    pallas_call x1, Pallas kernels, shards(): pl.pallas_call(far_kernel, out_shape=jax.ShapeDtypeStruct((N, points), F3...  12.2 us
    all_to_all x1, starting transfers between devices, shards(): lax.all_to_all(message, both, split_axis=0, concat_axis=0, tiled=True)  12.2 us
    pallas_call x1, Pallas kernels, shards(): pl.pallas_call(moment_kernel, out_shape=jax.ShapeDtypeStruct((OWN * 4 * N...  9.44 us
    ppermute x2, starting transfers between devices, swapped(): lax.ppermute(block, axis, [(i, i + 1) for i in lower] + [(i + 1, i) for i...  3.19 us
    pallas_call x1, Pallas kernels, shards(): pl.pallas_call(pack_kernel, out_shape=(jax.ShapeDtypeStruct((2 * N, rim),...  2.72 us
  transfers between devices with their start and end apart: 3, of which 0 were waited for; matrix products, arithmetic and copies ran while one was open for 0% of the time, Pallas kernels for 65%

profile of v6, /device:TPU:4, one launch (start us, length us, event | category | flops | bytes accessed | tf_op | source)
XLA Modules:
  0.0 89.8 jit_solution(15622850013657917854)
XLA Ops:
  0.0 2.7 %pack.1 = (bf16[16,16384]{1,0:T(8,128)(2,1)}, bf16[16,16384]{1,0:T(8,128)(2,1)}) custom-call(s32[1]{0:T(128)} %bitcast.place, f32[3,32768]{1,0:T(4,128)} %points_hbm.3, f32[8,32768]{1,0:T(8,128)} %values_hbm.5), custom_call_target="tpu_custom_call" | custom-call | flops 10000000 | bytes 3145728 | tf_op jit(solution)/shard_map/pack/pallas_call | solution.py:378
  2.7 1.3 %collective-permute-start = (bf16[16,16384]{1,0:T(8,128)(2,1)}, bf16[16,16384]{1,0:T(8,128)(2,1)S(1)}, u32[]{:S(2)}, u32[]{:S(2)}) collective-permute-start(bf16[16,16384]{1,0:T(8,128)(2,1)} %get-tuple-element.7), channel_id=1, source_target_pairs={{0,1},{2,3},{4,5},{6,7},{8,9},{10,11},{12,13},{14,15},{16,17},{18,... | collective-permute-start | bytes 1572872 | tf_op jit(solution)/shard_map/ppermute | solution.py:366
  4.0 1.9 %collective-permute-start.1 = (bf16[16,16384]{1,0:T(8,128)(2,1)}, bf16[16,16384]{1,0:T(8,128)(2,1)}, u32[]{:S(2)}, u32[]{:S(2)}) collective-permute-start(bf16[16,16384]{1,0:T(8,128)(2,1)} %get-tuple-element.8), channel_id=1, source_target_pairs={{1,2},{3,4},{5,6},{7,8},{9,10},{11,12},{13,14},{15,16},{17,18},{19... | collective-permute-start | bytes 1572872 | tf_op jit(solution)/shard_map/ppermute | solution.py:366
  5.9 9.4 %moments.1 = bf16[4096,128]{1,0:T(8,128)(2,1)} custom-call(s32[1]{0:T(128)} %bitcast.place, s32[6,1,128]{2,1,0:T(1,128)} %bitcast.9, s32[1,128]{1,0:T(1,128)} %send_count.1, f32[8,32768]{1,0:T(8,128)} %values_hbm.5, bf16[128,64,256]{2,1,0:T(8,128)(2,1)} %basis_hbm.3, bf16[64,8192]{1,0:T(8,128)(2,1)} %transfer_hbm.3, f32[254,4096]{1,0:T(8,128)} %top_transfer_hbm.3), custom_call_target="tpu_custom_call" | custom-call | flops 1000000000 | bytes 12582912 | tf_op jit(solution)/shard_map/moments/pallas_call | solution.py:391
  15.4 12.2 %all-to-all-start = ((bf16[128,32,128]{2,1,0:T(8,128)(2,1)}), bf16[128,32,128]{2,1,0:T(8,128)(2,1)}, u32[]{:S(2)}, u32[]{:S(2)}) async-start(bf16[128,32,128]{2,1,0:T(8,128)(2,1)} %bitcast.8), calls=%async_computation | async-start | bytes 2097152 | tf_op jit(solution)/shard_map/all_to_all | solution.py:410
  27.6 0.0 collective-permute-done.first
  27.6 0.0 copy-start
  27.6 0.0 collective-permute-done.1.second
  27.6 0.8 copy-done
  28.4 49.0 %near.1.near_hbm = f32[8,32768]{1,0:T(8,128)} custom-call(s32[1]{0:T(128)} %bitcast.place, s32[6,128]{1,0:T(8,128)} %bitcast.11, bf16[16,16384]{1,0:T(8,128)(2,1)} %copy-done, bf16[16,16384]{1,0:T(8,128)(2,1)} %collective-permute-done.1.second, f32[3,32768]{1,0:T(4,128)} %points_hbm.3, f32[8,32768]{1,0:T(8,128)} %values_hbm.5), custom_call_target="tpu_custom_call" | custom-call | flops 60000002048 | bytes 6291456 | tf_op jit(solution)/shard_map/near/pallas_call | solution.py:412
  77.4 0.0 all-to-all-done
  77.4 12.2 %far_field.1 = f32[8,32768]{1,0:T(8,128)} custom-call(s32[1]{0:T(128)} %bitcast.place, s32[6,1,128]{2,1,0:T(1,128)} %bitcast.10, bf16[4096,128]{1,0:T(8,128)(2,1)} %bitcast.4.incoming, f32[8,32768]{1,0:T(8,128)} %near.1.near_hbm, bf16[128,64,384]{2,1,0:T(8,128)(2,1)} %bitcast.7, bf16[64,8192]{1,0:T(8,128)(2,1)} %transfer_hbm.3, ...), custom_call_target="tpu_custom_call" | custom-call | flops 2000000000 | bytes 23068672 | tf_op jit(solution)/shard_map/far_field/pallas_call | solution.py:430
Async XLA Ops:
  2.7 24.8 %collective-permute-start = (bf16[16,16384]{1,0:T(8,128)(2,1)}, bf16[16,16384]{1,0:T(8,128)(2,1)S(1)}, u32[]{:S(2)}, u32[]{:S(2)}) collective-permute-start(bf16[16,16384]{1,0:T(8,128)(2,1)} %get-tuple-element.7), channel_id=1, source_target_pairs={{0,1},{2,3},{4,5},{6,7},{8,9},{10,11},{12,13},{14,15},{16,17},{18,... | collective-permute-start | bytes 1572872 | tf_op jit(solution)/shard_map/ppermute | solution.py:366
  4.0 23.6 %collective-permute-start.1 = (bf16[16,16384]{1,0:T(8,128)(2,1)}, bf16[16,16384]{1,0:T(8,128)(2,1)}, u32[]{:S(2)}, u32[]{:S(2)}) collective-permute-start(bf16[16,16384]{1,0:T(8,128)(2,1)} %get-tuple-element.8), channel_id=1, source_target_pairs={{1,2},{3,4},{5,6},{7,8},{9,10},{11,12},{13,14},{15,16},{17,18},{19... | collective-permute-start | bytes 1572872 | tf_op jit(solution)/shard_map/ppermute | solution.py:366
  15.4 62.0 %all-to-all-start = ((bf16[128,32,128]{2,1,0:T(8,128)(2,1)}), bf16[128,32,128]{2,1,0:T(8,128)(2,1)}, u32[]{:S(2)}, u32[]{:S(2)}) async-start(bf16[128,32,128]{2,1,0:T(8,128)(2,1)} %bitcast.8), calls=%async_computation | async-start | bytes 2097152 | tf_op jit(solution)/shard_map/all_to_all | solution.py:410
  27.6 0.8 copy-start
